TPU v7x, 128 devices: a whole 4x4x4 slice. The times are simulated.
128 devices in a mesh: region: 16 (over z, x), sub: 8 (over y, core).
Axes of the slice: x: 4, y: 4, z: 4, core: 2. Of those that a mesh axis runs over, the one named last changes fastest.
Arguments:
- nodes: bfloat16 [65536, 512], P(('region', 'sub')), may hold values from -6 to 6
- edges: bfloat16 [393216, 512], P(('region', 'sub')), may hold values from -6 to 6
- sender: int32 [393216], P(('region', 'sub')), may hold values from 0 to 1247, as said below
- receiver: int32 [393216], P(('region', 'sub')), may hold values from 0 to 511, as said below
- tile_counts: int32 [1536], P(('region', 'sub')), may hold values from 64 to 256, as said below
- send_list: int32 [128, 736], P(('region', 'sub')), may hold values from 0 to 511, as said below
- edge_w1: bfloat16 [1536, 512], replicated, may hold values from -0.15625 to 0.15625
- edge_w2: bfloat16 [512, 512], replicated, may hold values from -0.25 to 0.25
- edge_gain: float32 [512], replicated, may hold values from 0.5 to 1.5
- node_w1: bfloat16 [1024, 512], replicated, may hold values from -0.1875 to 0.1875
- node_w2: bfloat16 [512, 512], replicated, may hold values from -0.25 to 0.25
- node_gain: float32 [512], replicated, may hold values from 0.5 to 1.5
- node_cotangent: bfloat16 [65536, 512], P(('region', 'sub')), may hold values from -6 to 6
- edge_cotangent: bfloat16 [393216, 512], P(('region', 'sub')), may hold values from -6 to 6
Outputs:
- edge_out: bfloat16 [393216, 512], P(('region', 'sub'))
- node_out: bfloat16 [65536, 512], P(('region', 'sub'))
- grad_edges: bfloat16 [393216, 512], P(('region', 'sub'))
- grad_nodes: bfloat16 [65536, 512], P(('region', 'sub'))
Inputs may be any that keep to these rules, and one draw needn't show every extreme that they name: `sender`: below 512: a node of the edge's own block b. 512 + o * 80 + s for o below 6: slot s of the rows that block b - d_o (modulo the number of blocks; d = 1, 2, 3, -1, -2, -3) sends to block b. 512 + 6 * 80 + p * 2 + s: slot s of the rows that block p sends to block b. Each value from 512 upward is taken by exactly one live edge of each block. `receiver`: Non-decreasing within each block of 3072 edges; 0 and 511 occur in every block. `tile_counts`: every block has a full tile. `send_list`: row b: positions o * 80 to o * 80 + 79, local nodes of block b sent to block b + d_o (modulo the number of blocks); positions 480 + p * 2 to 480 + p * 2 + 1, local nodes of block b sent to block p; a node may appear several times.
All inputs are finite; a program needn't handle non-finite values.
Results may differ from a plain program's by a relative error of at most 0.015.
Values may be sent and summed in bfloat16 or wider, within the bound.
No kernel may reach another device: no remote copies, remote signals or barrier semaphores. Data moves between devices by JAX's collectives and lax.ppermute only.
A program may use at most 192 MiB of HBM per device.

v0:
```python
import functools

import jax
import jax.numpy as jnp
from jax import lax
from jax.experimental import pallas as pl
from jax.experimental.pallas import tpu as pltpu
from jax.sharding import PartitionSpec as P

NEAR = 80
NEAR_TOTAL = 480
TILE = 256
BF = jnp.bfloat16
F32 = jnp.float32
AXES = ("region", "sub")
VMEM = pltpu.VMEM
MIB = 1024 * 1024


def near_offset(neighbour):
    return neighbour + 1 if neighbour < 3 else 2 - neighbour


def shifted(value, steps):
    count = lax.axis_size(AXES)
    return lax.ppermute(value, AXES, [(s, (s + steps) % count) for s in range(count)])


def exchange_far(rows):
    return lax.all_to_all(rows, AXES, split_axis=0, concat_axis=0, tiled=True)


def dot(a, b):
    return lax.dot_general(a, b, (((1,), (0,)), ((), ())), preferred_element_type=F32)


def dot_nt(a, b):
    return lax.dot_general(a, b, (((1,), (1,)), ((), ())), preferred_element_type=F32)


def dot_tn(a, b):
    return lax.dot_general(a, b, (((0,), (0,)), ((), ())), preferred_element_type=F32)


def hot_rows(index_row, first, count):
    ids = lax.broadcasted_iota(jnp.int32, (count, index_row.shape[1]), 0) + first
    return jnp.where(ids == index_row, 1.0, 0.0).astype(BF)


def hot_columns(index_lanes, first, count):
    lane = lax.broadcasted_iota(jnp.int32, index_lanes.shape, 1) + first
    parts = [
        jnp.where(index_lanes == lane + 128 * k, 1.0, 0.0).astype(BF) for k in range(count // 128)
    ]
    return jnp.concatenate(parts, axis=1)


def spread_lanes(index_ref, lanes_ref):
    flipped = jnp.transpose(index_ref[...], (1, 0))
    for j in range(index_ref.shape[0]):
        lanes_ref[pl.ds(j * 128, 128), :] = jnp.broadcast_to(flipped[:, j : j + 1], (128, 128))


def row_mean(x):
    return jnp.sum(x, axis=1, keepdims=True) * (1.0 / x.shape[1])


def normalise(mixed):
    centre = mixed - row_mean(mixed)
    spread = lax.rsqrt(row_mean(centre * centre) + 1e-05)
    return centre * spread, spread


def norm_back(scaled, normal, spread):
    return spread * (scaled - row_mean(scaled) - normal * row_mean(scaled * normal))


def sigmoid(x):
    return 1.0 / (1.0 + jnp.exp(-x))


def slope_of(hidden, sigma):
    return sigma * (1.0 + hidden * (1.0 - sigma))


def tile_rows(t):
    return pl.ds(pl.multiple_of(t * TILE, TILE), TILE)


def copies_of(tiles, src, dst, sems):
    return [
        pltpu.make_async_copy(src.at[tile_rows(t)], dst.at[tile_rows(t)], sems.at[t])
        for t in range(tiles)
    ]


def copy_of(t, src, dst, sems):
    return pltpu.make_async_copy(src.at[tile_rows(t)], dst.at[tile_rows(t)], sems.at[t])


def gather_kernel(nodes_ref, list_ref, *outs):
    hot = hot_rows(list_ref[...], 0, nodes_ref.shape[0])
    rows = dot_tn(hot, nodes_ref[...]).astype(BF)
    for i in range(6):
        outs[i][...] = rows[i * NEAR : (i + 1) * NEAR]
    outs[6][...] = rows[NEAR_TOTAL:]


def local_kernel(
    nodes_ref, sender_ref, receiver_ref, w1_ref, edges_hbm, part_hbm,
    edges, part, slanes, rlanes, table, in_sem, out_sem,
):
    tiles = edges.shape[0] // TILE
    width = nodes_ref.shape[1]
    count = nodes_ref.shape[0]
    for c in copies_of(tiles, edges_hbm, edges, in_sem):
        c.start()
    spread_lanes(sender_ref, slanes)
    spread_lanes(receiver_ref, rlanes)
    nodes = nodes_ref[...]
    table[:count, :] = dot(nodes, w1_ref[width : 2 * width, :]).astype(BF)
    table[count:, :] = dot(nodes, w1_ref[2 * width :, :]).astype(BF)

    def body(t, carry):
        rows = tile_rows(t)
        hot = jnp.concatenate(
            [hot_columns(slanes[rows, :], 0, count), hot_columns(rlanes[rows, :], 0, count)], axis=1
        )
        total = dot(hot, table[...])
        copy_of(t, edges_hbm, edges, in_sem).wait()
        total = total + dot(edges[rows, :], w1_ref[:width, :])
        part[rows, :] = total.astype(BF)
        copy_of(t, part, part_hbm, out_sem).start()
        return carry

    lax.fori_loop(0, tiles, body, 0)
    for c in copies_of(tiles, part, part_hbm, out_sem):
        c.wait()


def main_kernel(
    counts_ref, n0, n1, n2, n3, n4, n5, far_ref, sender_ref, receiver_ref, srow_ref, rrow_ref,
    w1s_ref, w2_ref, gain_ref, nw1_ref, nw2_ref, ngain_ref, nodes_ref, ncot_ref,
    part_hbm, edges_hbm, cot_hbm,
    edge_out_hbm, node_out_ref, hgrad_hbm, r0, r1, r2, r3, r4, r5, rfar, direct_ref,
    part, edges, cot, normals, slopes, hgrad, slanes, rlanes, spreads, table, sums, aggregate,
    agrad, part_sem, edges_sem, cot_sem, eout_sem, hgrad_sem,
):
    tiles = edges.shape[0] // TILE
    count, width = nodes_ref.shape
    halo = table.shape[0]
    for t in range(tiles):
        copy_of(t, part_hbm, part, part_sem).start()
        copy_of(t, edges_hbm, edges, edges_sem).start()
    for c in copies_of(tiles, cot_hbm, cot, cot_sem):
        c.start()
    spread_lanes(sender_ref, slanes)
    spread_lanes(receiver_ref, rlanes)
    arrived = jnp.concatenate([r[...] for r in (n0, n1, n2, n3, n4, n5)] + [far_ref[...]], axis=0)
    table[: arrived.shape[0], :] = dot(arrived, w1s_ref[...]).astype(BF)
    table[arrived.shape[0] :, :] = jnp.zeros((halo - arrived.shape[0], width), BF)
    aggregate[...] = jnp.zeros_like(aggregate)
    sums[...] = jnp.zeros_like(sums)
    gain = gain_ref[...]
    position = lax.broadcasted_iota(jnp.int32, (TILE, 1), 0)

    def forward(t, carry):
        rows = tile_rows(t)
        hot = hot_columns(slanes[rows, :], count, halo)
        remote = dot(hot, table[...])
        copy_of(t, part_hbm, part, part_sem).wait()
        hidden = part[rows, :].astype(F32) + remote
        sigma = sigmoid(hidden)
        slopes[rows, :] = slope_of(hidden, sigma).astype(BF)
        mixed = dot((hidden * sigma).astype(BF), w2_ref[...])
        normal, spread = normalise(mixed)
        normals[rows, :] = normal.astype(BF)
        spreads[rows, :] = spread
        live = (position < counts_ref[t]).astype(F32)
        message = normal * gain * live
        copy_of(t, edges_hbm, edges, edges_sem).wait()
        edges[rows, :] = (edges[rows, :].astype(F32) + message).astype(BF)
        copy_of(t, edges, edge_out_hbm, eout_sem).start()
        into = hot_rows(rrow_ref[t], 0, count)
        aggregate[...] += dot(into, message.astype(BF))
        return carry

    lax.fori_loop(0, tiles, forward, 0)

    nodes = nodes_ref[...]
    node_hidden = dot(nodes, nw1_ref[:width, :]) + dot(aggregate[...].astype(BF), nw1_ref[width:, :])
    sigma = sigmoid(node_hidden)
    node_slope = slope_of(node_hidden, sigma)
    node_mixed = dot((node_hidden * sigma).astype(BF), nw2_ref[...])
    normal, spread = normalise(node_mixed)
    node_out_ref[...] = (nodes.astype(F32) + normal * ngain_ref[...]).astype(BF)
    node_cot = ncot_ref[...].astype(F32)
    mixed_grad = norm_back(node_cot * ngain_ref[...], normal, spread).astype(BF)
    hidden_grad = (dot_nt(mixed_grad, nw2_ref[...]) * node_slope).astype(BF)
    direct_ref[...] = node_cot + dot_nt(hidden_grad, nw1_ref[:width, :])
    agrad[...] = dot_nt(hidden_grad, nw1_ref[width:, :]).astype(BF)

    def backward(t, carry):
        rows = tile_rows(t)
        upper = dot(hot_columns(rlanes[rows, :], 0, count), agrad[...])
        copy_of(t, cot_hbm, cot, cot_sem).wait()
        live = (position < counts_ref[t]).astype(F32)
        scaled = (upper + cot[rows, :].astype(F32)) * gain * live
        grad = norm_back(scaled, normals[rows, :].astype(F32), spreads[rows, :]).astype(BF)
        hg = (dot_nt(grad, w2_ref[...]) * slopes[rows, :].astype(F32)).astype(BF)
        hgrad[rows, :] = hg
        copy_of(t, hgrad, hgrad_hbm, hgrad_sem).start()
        sums[...] += dot(hot_rows(srow_ref[t], count, halo), hg)
        return carry

    lax.fori_loop(0, tiles, backward, 0)
    back = dot_nt(sums[...].astype(BF), w1s_ref[...]).astype(BF)
    for i, ref in enumerate((r0, r1, r2, r3, r4, r5)):
        ref[...] = back[i * NEAR : (i + 1) * NEAR]
    rfar[...] = back[NEAR_TOTAL : NEAR_TOTAL + rfar.shape[0]]
    for c in copies_of(tiles, edges, edge_out_hbm, eout_sem):
        c.wait()
    for c in copies_of(tiles, hgrad, hgrad_hbm, hgrad_sem):
        c.wait()


def rest_kernel(
    srow_ref, rrow_ref, w1_ref, direct_ref, hgrad_hbm, cot_hbm, grad_hbm, owned_ref,
    hgrad, cot, sums, h_sem, c_sem, out_sem,
):
    tiles = hgrad.shape[0] // TILE
    count, width = direct_ref.shape
    for t in range(tiles):
        copy_of(t, hgrad_hbm, hgrad, h_sem).start()
        copy_of(t, cot_hbm, cot, c_sem).start()
    sums[...] = jnp.zeros_like(sums)

    def body(t, carry):
        rows = tile_rows(t)
        copy_of(t, hgrad_hbm, hgrad, h_sem).wait()
        copy_of(t, cot_hbm, cot, c_sem).wait()
        hg = hgrad[rows, :]
        cot[rows, :] = (cot[rows, :].astype(F32) + dot_nt(hg, w1_ref[:width, :])).astype(BF)
        copy_of(t, cot, grad_hbm, out_sem).start()
        sums[:count, :] += dot(hot_rows(srow_ref[t], 0, count), hg)
        sums[count:, :] += dot(hot_rows(rrow_ref[t], 0, count), hg)
        return carry

    lax.fori_loop(0, tiles, body, 0)
    owned_ref[...] = (
        direct_ref[...]
        + dot_nt(sums[:count, :].astype(BF), w1_ref[width : 2 * width, :])
        + dot_nt(sums[count:, :].astype(BF), w1_ref[2 * width :, :])
    )
    for c in copies_of(tiles, cot, grad_hbm, out_sem):
        c.wait()


def final_kernel(list_ref, owned_ref, n0, n1, n2, n3, n4, n5, far_ref, out_ref):
    returned = jnp.concatenate([r[...] for r in (n0, n1, n2, n3, n4, n5)] + [far_ref[...]], axis=0)
    hot = hot_rows(list_ref[...], 0, owned_ref.shape[0])
    out_ref[...] = (owned_ref[...] + dot(hot, returned)).astype(BF)


def kernel_call(body, outs, in_specs, out_specs, scratch, flops, moved, limit):
    return pl.pallas_call(
        body,
        out_shape=outs,
        in_specs=in_specs,
        out_specs=out_specs,
        scratch_shapes=scratch,
        compiler_params=pltpu.CompilerParams(vmem_limit_bytes=limit * MIB),
        cost_estimate=pl.CostEstimate(flops=flops, bytes_accessed=moved, transcendentals=0),
    )


def on_device(
    nodes, edges, sender, receiver, tile_counts, send_list, edge_w1, edge_w2, edge_gain,
    node_w1, node_w2, node_gain, node_cotangent, edge_cotangent,
):
    count, width = nodes.shape
    slots = edges.shape[0]
    tiles = slots // TILE
    halo = send_list.shape[1]
    far_rows = halo - NEAR_TOTAL
    padded = -(-halo // 256) * 256
    v = pl.BlockSpec(memory_space=pltpu.VMEM)
    s = pl.BlockSpec(memory_space=pltpu.SMEM)
    a = pl.BlockSpec(memory_space=pl.ANY)
    sds = jax.ShapeDtypeStruct
    sem = pltpu.SemaphoreType.DMA((tiles,))
    near_shapes = [sds((NEAR, width), BF)] * 6 + [sds((far_rows, width), BF)]
    big = sds((slots, width), BF)
    wide = VMEM((slots, width), BF)
    lanes = VMEM((slots, 128), jnp.int32)
    square = 2 * count * width * width

    sender_lanes = sender.reshape(slots // 128, 128)
    receiver_lanes = receiver.reshape(slots // 128, 128)
    sender_rows = sender.reshape(tiles, 1, TILE)
    receiver_rows = receiver.reshape(tiles, 1, TILE)
    gain = edge_gain.reshape(1, width)
    ngain = node_gain.reshape(1, width)

    leaving = kernel_call(
        gather_kernel, near_shapes, [v, v], [v] * 7, [], 2 * halo * count * width, 2 * MIB, 16
    )(nodes, send_list)
    arrived = [shifted(leaving[i], near_offset(i)) for i in range(6)]
    far = exchange_far(leaving[6])

    part = kernel_call(
        local_kernel, big, [v, v, v, v, a], a,
        [wide, wide, lanes, lanes, VMEM((2 * count, width), BF), sem, sem],
        20 * square, 8 * MIB, 24,
    )(nodes, sender_lanes, receiver_lanes, edge_w1, edges)

    outs = kernel_call(
        main_kernel,
        [big, sds((count, width), BF), big] + near_shapes + [sds((count, width), F32)],
        [s] + [v] * 19 + [a] * 3,
        [a, v, a] + [v] * 8,
        [wide] * 6
        + [lanes, lanes, VMEM((slots, 1), F32), VMEM((padded, width), BF), VMEM((padded, width), F32),
           VMEM((count, width), F32), VMEM((count, width), BF)]
        + [sem] * 5,
        50 * square, 20 * MIB, 48,
    )(
        tile_counts, *arrived, far, sender_lanes, receiver_lanes, sender_rows, receiver_rows,
        edge_w1[width : 2 * width], edge_w2, gain, node_w1, node_w2, ngain, nodes, node_cotangent,
        part, edges, edge_cotangent,
    )
    edge_out, node_out, hgrad = outs[:3]
    back = outs[3:10]
    direct = outs[10]
    returned = [shifted(back[i], -near_offset(i)) for i in range(6)]
    far_back = exchange_far(back[6])

    grad_edges, owned = kernel_call(
        rest_kernel, [big, sds((count, width), F32)], [v] * 4 + [a, a], [a, v],
        [wide, wide, VMEM((2 * count, width), F32), sem, sem, sem],
        20 * square, 12 * MIB, 24,
    )(sender_rows, receiver_rows, edge_w1, direct, hgrad, edge_cotangent)

    grad_nodes = kernel_call(
        final_kernel, sds((count, width), BF), [v] * 9, v, [], 2 * square, 3 * MIB, 16
    )(send_list, owned, *returned, far_back)
    return edge_out, node_out, grad_edges, grad_nodes


def solution(mesh):
    rows = P(AXES, None)
    flat = P(AXES)
    in_specs = (
        rows, rows, flat, flat, flat, rows, P(), P(), P(), P(), P(), P(), rows, rows,
    )
    return jax.shard_map(
        on_device, mesh=mesh, in_specs=in_specs, out_specs=(rows,) * 4, check_vma=False
    )
```

profile of v0, /device:TPU:1, one launch (start us, length us, event | category | flops | bytes accessed | tf_op | source)
XLA Modules:
  0.0 131.3 jit_solution(13637506273547709748)
XLA Ops:
  0.6 0.0 copy-start.2
  0.6 0.7 copy-done.2
  1.3 1.0 copy-done.6
  2.4 0.6 shard_map.165
  3.0 2.8 %collective-permute-start = (bf16[80,512]{1,0:T(8,128)(2,1)S(1)}, bf16[80,512]{1,0:T(8,128)(2,1)S(1)}, u32[]{:S(2)}, u32[]{:S(2)}) collective-permute-start(bf16[80,512]{1,0:T(8,128)(2,1)S(1)} %get-tuple-element.24), channel_id=1, source_target_pairs={{0,1},{1,2},{2,3},{3,4},{4,5},{5,6},{6,7},{7,8},{8,9},{9,10},{10,1... | collective-permute-start | bytes 245768 | tf_op jit(solution)/shard_map/ppermute | solution.py:26
  5.7 1.3 collective-permute-start.1
  7.0 1.7 %collective-permute-start.2 = (bf16[80,512]{1,0:T(8,128)(2,1)S(1)}, bf16[80,512]{1,0:T(8,128)(2,1)S(1)}, u32[]{:S(2)}, u32[]{:S(2)}) collective-permute-start(bf16[80,512]{1,0:T(8,128)(2,1)S(1)} %get-tuple-element.26), channel_id=1, source_target_pairs={{0,3},{1,4},{2,5},{3,6},{4,7},{5,8},{6,9},{7,10},{8,11},{9,12},{10... | collective-permute-start | bytes 245768 | tf_op jit(solution)/shard_map/ppermute | solution.py:26
  8.7 0.0 collective-permute-start.3
  8.7 5.6 %collective-permute-start.4 = (bf16[80,512]{1,0:T(8,128)(2,1)S(1)}, bf16[80,512]{1,0:T(8,128)(2,1)S(1)}, u32[]{:S(2)}, u32[]{:S(2)}) collective-permute-start(bf16[80,512]{1,0:T(8,128)(2,1)S(1)} %get-tuple-element.28), channel_id=1, source_target_pairs={{0,126},{1,127},{2,0},{3,1},{4,2},{5,3},{6,4},{7,5},{8,6},{9,7},{1... | collective-permute-start | bytes 245768 | tf_op jit(solution)/shard_map/ppermute | solution.py:26
  14.3 0.8 all_to_all.14
  15.1 5.6 %all-to-all-start = ((bf16[128,2,512]{2,1,0:T(2,128)(2,1)}), bf16[128,2,512]{2,1,0:T(2,128)(2,1)S(1)}, u32[]{:S(2)}, u32[]{:S(2)}) async-start(bf16[128,2,512]{2,1,0:T(2,128)(2,1)} %all_to_all.14), calls=%async_computation | async-start | bytes 524288 | tf_op jit(solution)/shard_map/all_to_all | solution.py:30
  20.7 0.0 collective-permute-done.n0
  20.7 8.0 %collective-permute-start.5 = (bf16[80,512]{1,0:T(8,128)(2,1)S(1)}, bf16[80,512]{1,0:T(8,128)(2,1)S(1)}, u32[]{:S(2)}, u32[]{:S(2)}) collective-permute-start(bf16[80,512]{1,0:T(8,128)(2,1)S(1)} %get-tuple-element.29), channel_id=1, source_target_pairs={{0,125},{1,126},{2,127},{3,0},{4,1},{5,2},{6,3},{7,4},{8,5},{9,6},... | collective-permute-start | bytes 245768 | tf_op jit(solution)/shard_map/ppermute | solution.py:26
  28.7 1.4 %copy-done = bf16[1536,512]{1,0:T(8,128)(2,1)S(1)} copy-done((bf16[1536,512]{1,0:T(8,128)(2,1)S(1)}, bf16[1536,512]{1,0:T(8,128)(2,1)}, u32[]{:S(2)}) %copy-start) | copy-done | bytes 1572888
  30.2 1.9 %copy-done.4 = bf16[3072,512]{1,0:T(8,128)(2,1)S(1)} copy-done((bf16[3072,512]{1,0:T(8,128)(2,1)S(1)}, bf16[3072,512]{1,0:T(8,128)(2,1)}, u32[]{:S(2)}) %copy-start.4) | copy-done | bytes 3145752
  32.0 1.0 copy-done.7
  33.1 0.7 copy-done.20
  33.8 0.7 copy-done.23
  34.5 10.3 %shard_map.166.part_hbm = bf16[3072,512]{1,0:T(8,128)(2,1)S(1)} custom-call(bf16[512,512]{1,0:T(8,128)(2,1)S(1)} %copy-done.7, s32[24,128]{1,0:T(8,128)S(1)} %bitcast.6, s32[24,128]{1,0:T(8,128)S(1)} %bitcast.10, bf16[1536,512]{1,0:T(8,128)(2,1)S(1)} %copy-done, bf16[3072,512]{1,0:T(8,128)(2,1)S(1)} %copy-done.4), custom_call_target="tpu_custom_call" | custom-call | flops 5368709120 | bytes 8388608 | tf_op jit(solution)/shard_map/pallas_call | solution.py:311
  44.8 0.0 copy-start.30
  44.8 1.7 %copy-done.30 = bf16[3072,512]{1,0:T(8,128)(2,1)} copy-done((bf16[3072,512]{1,0:T(8,128)(2,1)}, bf16[3072,512]{1,0:T(8,128)(2,1)S(1)}, u32[]{:S(2)}) %copy-start.30) | copy-done | bytes 3145752
  46.5 0.1 all_to_all.16.far_ref
  46.6 0.0 copy-start.12
  46.6 0.6 copy-done.12
  47.3 0.0 collective-permute-done.3.n3
  47.3 0.6 copy-done.14
  47.9 0.0 collective-permute-done.4.n4
  47.9 0.6 copy-done.16
  48.5 0.6 copy-done.18
  49.2 1.0 copy-done.9
  50.2 1.0 copy-done.10
  51.3 1.0 copy-done.11
  52.3 0.9 copy-done.13
  53.2 0.9 copy-done.15
  54.1 0.9 copy-done.17
  55.0 0.9 copy-done.19
  55.9 0.7 copy-done.21
  56.6 0.7 copy-done.24
  57.3 0.7 copy-done.26
  58.0 0.7 copy-done.27
  58.6 0.7 copy-done.28
  59.3 36.3 %shard_map.167 = (bf16[3072,512]{1,0:T(8,128)(2,1)}, bf16[512,512]{1,0:T(8,128)(2,1)}, bf16[3072,512]{1,0:T(8,128)(2,1)}, bf16[80,512]{1,0:T(8,128)(2,1)}, bf16[...) custom-call(s32[12]{0:T(128)S(1)} %copy-done.28, ...), custom_call_target="tpu_custom_call" | custom-call | flops 13421772800 | bytes 20971520 | tf_op jit(solution)/shard_map/pallas_call | solution.py:317
  95.6 0.0 copy-start.31
  95.6 1.0 copy-done.31
  96.5 0.4 collective-permute-start.6
  96.9 0.8 collective-permute-start.7
  97.7 0.3 collective-permute-start.8
  98.1 1.0 collective-permute-start.9
  99.1 1.6 %collective-permute-start.10 = (bf16[80,512]{1,0:T(8,128)(2,1)S(1)}, bf16[80,512]{1,0:T(8,128)(2,1)S(1)}, u32[]{:S(2)}, u32[]{:S(2)}) collective-permute-start(bf16[80,512]{1,0:T(8,128)(2,1)S(1)} %get-tuple-element.41), channel_id=1, source_target_pairs={{0,2},{1,3},{2,4},{3,5},{4,6},{5,7},{6,8},{7,9},{8,10},{9,11},{10,... | collective-permute-start | bytes 245768 | tf_op jit(solution)/shard_map/ppermute | solution.py:26
  100.7 0.8 all_to_all.17
  101.5 8.7 %all-to-all-start.1 = ((bf16[128,2,512]{2,1,0:T(2,128)(2,1)}), bf16[128,2,512]{2,1,0:T(2,128)(2,1)}, u32[]{:S(2)}, u32[]{:S(2)}) async-start(bf16[128,2,512]{2,1,0:T(2,128)(2,1)} %all_to_all.17), calls=%async_computation.1 | async-start | bytes 524288 | tf_op jit(solution)/shard_map/all_to_all | solution.py:30
  110.2 3.2 %collective-permute-start.11 = (bf16[80,512]{1,0:T(8,128)(2,1)S(1)}, bf16[80,512]{1,0:T(8,128)(2,1)S(1)}, u32[]{:S(2)}, u32[]{:S(2)}) collective-permute-start(bf16[80,512]{1,0:T(8,128)(2,1)S(1)} %get-tuple-element.42), channel_id=1, source_target_pairs={{0,3},{1,4},{2,5},{3,6},{4,7},{5,8},{6,9},{7,10},{8,11},{9,12},{10... | collective-permute-start | bytes 245768 | tf_op jit(solution)/shard_map/ppermute | solution.py:26
  113.4 1.9 %copy-done.5 = bf16[3072,512]{1,0:T(8,128)(2,1)S(1)} copy-done((bf16[3072,512]{1,0:T(8,128)(2,1)S(1)}, bf16[3072,512]{1,0:T(8,128)(2,1)}, u32[]{:S(2)}) %copy-start.5) | copy-done | bytes 3145752
  115.3 0.7 copy-done.22
  116.0 0.7 copy-done.25
  116.8 1.9 %copy-done.29 = bf16[3072,512]{1,0:T(8,128)(2,1)S(1)} copy-done((bf16[3072,512]{1,0:T(8,128)(2,1)S(1)}, bf16[3072,512]{1,0:T(8,128)(2,1)}, u32[]{:S(2)}) %copy-start.29) | copy-done | bytes 3145752
  118.6 1.2 copy-done.32
  119.9 9.0 %shard_map.168 = (bf16[3072,512]{1,0:T(8,128)(2,1)}, f32[512,512]{1,0:T(8,128)S(1)}) custom-call(s32[12,1,256]{2,1,0:T(1,128)S(1)} %bitcast.9, s32[12,1,256]{2,1,0:T(1,128)S(1)} %bitcast.13, bf16[1536,512]{1,0:T(8,128)(2,1)S(1)} %copy-done.1, f32[512,512]{1,0:T(8,128)S(1)} %copy-done.32, bf16[3072,512]{1,0:T(8,128)(2,1)S(1)} %copy-done.29, ...), custom_call_target="tpu_custom_call" | custom-call | flops 5368709120 | bytes 12582912 | tf_op jit(solution)/shard_map/pallas_call | solution.py:338
  128.8 0.0 all-to-all-done.1
  128.9 1.1 all_to_all.19.far_ref
  129.9 0.0 collective-permute-done.7.n1
  129.9 0.0 collective-permute-done.9.n3
  129.9 0.0 collective-permute-done.10.n4
  130.0 1.4 %shard_map.169 = bf16[512,512]{1,0:T(8,128)(2,1)} custom-call(s32[1,736]{1,0:T(1,128)S(1)} %copy-done.3, f32[512,512]{1,0:T(8,128)S(1)} %get-tuple-element.36.owned_ref, bf16[80,512]{1,0:T(8,128)(2,1)S(1)} %collective-permute-done.6.n0, bf16[80,512]{1,0:T(8,128)(2,1)S(1)} %collective-permute-done.7.n1, bf16[80,512]{1,0:T(8,128)(2,1)S(1)} %collective-permute-done.8.n2, ...), custom_call_target="tpu_custom_call" | custom-call | flops 536870912 | bytes 3145728 | tf_op jit(solution)/shard_map/pallas_call | solution.py:344
  (40 shorter events, 0.1 us)
Async XLA Ops:
  0.6 0.7 copy-start.2
  1.3 1.0 copy-start.6
  3.0 17.7 %collective-permute-start = (bf16[80,512]{1,0:T(8,128)(2,1)S(1)}, bf16[80,512]{1,0:T(8,128)(2,1)S(1)}, u32[]{:S(2)}, u32[]{:S(2)}) collective-permute-start(bf16[80,512]{1,0:T(8,128)(2,1)S(1)} %get-tuple-element.24), channel_id=1, source_target_pairs={{0,1},{1,2},{2,3},{3,4},{4,5},{5,6},{6,7},{7,8},{8,9},{9,10},{10,1... | collective-permute-start | bytes 245768 | tf_op jit(solution)/shard_map/ppermute | solution.py:26
  5.7 40.9 %collective-permute-start.1 = (bf16[80,512]{1,0:T(8,128)(2,1)S(1)}, bf16[80,512]{1,0:T(8,128)(2,1)S(1)}, u32[]{:S(2)}, u32[]{:S(2)}) collective-permute-start(bf16[80,512]{1,0:T(8,128)(2,1)S(1)} %get-tuple-element.25), channel_id=1, source_target_pairs={{0,2},{1,3},{2,4},{3,5},{4,6},{5,7},{6,8},{7,9},{8,10},{9,11},{10,... | collective-permute-start | bytes 245768 | tf_op jit(solution)/shard_map/ppermute | solution.py:26
  7.0 39.6 %collective-permute-start.2 = (bf16[80,512]{1,0:T(8,128)(2,1)S(1)}, bf16[80,512]{1,0:T(8,128)(2,1)S(1)}, u32[]{:S(2)}, u32[]{:S(2)}) collective-permute-start(bf16[80,512]{1,0:T(8,128)(2,1)S(1)} %get-tuple-element.26), channel_id=1, source_target_pairs={{0,3},{1,4},{2,5},{3,6},{4,7},{5,8},{6,9},{7,10},{8,11},{9,12},{10... | collective-permute-start | bytes 245768 | tf_op jit(solution)/shard_map/ppermute | solution.py:26
  8.7 38.6 %collective-permute-start.3 = (bf16[80,512]{1,0:T(8,128)(2,1)S(1)}, bf16[80,512]{1,0:T(8,128)(2,1)S(1)}, u32[]{:S(2)}, u32[]{:S(2)}) collective-permute-start(bf16[80,512]{1,0:T(8,128)(2,1)S(1)} %get-tuple-element.27), channel_id=1, source_target_pairs={{0,127},{1,0},{2,1},{3,2},{4,3},{5,4},{6,5},{7,6},{8,7},{9,8},{10,... | collective-permute-start | bytes 245768 | tf_op jit(solution)/shard_map/ppermute | solution.py:26
  8.7 39.2 %collective-permute-start.4 = (bf16[80,512]{1,0:T(8,128)(2,1)S(1)}, bf16[80,512]{1,0:T(8,128)(2,1)S(1)}, u32[]{:S(2)}, u32[]{:S(2)}) collective-permute-start(bf16[80,512]{1,0:T(8,128)(2,1)S(1)} %get-tuple-element.28), channel_id=1, source_target_pairs={{0,126},{1,127},{2,0},{3,1},{4,2},{5,3},{6,4},{7,5},{8,6},{9,7},{1... | collective-permute-start | bytes 245768 | tf_op jit(solution)/shard_map/ppermute | solution.py:26
  15.1 31.4 %all-to-all-start = ((bf16[128,2,512]{2,1,0:T(2,128)(2,1)}), bf16[128,2,512]{2,1,0:T(2,128)(2,1)S(1)}, u32[]{:S(2)}, u32[]{:S(2)}) async-start(bf16[128,2,512]{2,1,0:T(2,128)(2,1)} %all_to_all.14), calls=%async_computation | async-start | bytes 524288 | tf_op jit(solution)/shard_map/all_to_all | solution.py:30
  20.7 27.8 %collective-permute-start.5 = (bf16[80,512]{1,0:T(8,128)(2,1)S(1)}, bf16[80,512]{1,0:T(8,128)(2,1)S(1)}, u32[]{:S(2)}, u32[]{:S(2)}) collective-permute-start(bf16[80,512]{1,0:T(8,128)(2,1)S(1)} %get-tuple-element.29), channel_id=1, source_target_pairs={{0,125},{1,126},{2,127},{3,0},{4,1},{5,2},{6,3},{7,4},{8,5},{9,6},... | collective-permute-start | bytes 245768 | tf_op jit(solution)/shard_map/ppermute | solution.py:26
  28.7 1.4 %copy-start = (bf16[1536,512]{1,0:T(8,128)(2,1)S(1)}, bf16[1536,512]{1,0:T(8,128)(2,1)}, u32[]{:S(2)}) copy-start(bf16[1536,512]{1,0:T(8,128)(2,1)} %w1_ref.3) | copy-start | bytes 4718596
  30.1 1.9 %copy-start.4 = (bf16[3072,512]{1,0:T(8,128)(2,1)S(1)}, bf16[3072,512]{1,0:T(8,128)(2,1)}, u32[]{:S(2)}) copy-start(bf16[3072,512]{1,0:T(8,128)(2,1)} %edges_hbm.3) | copy-start | bytes 9437188
  32.0 1.0 copy-start.7
  33.1 0.7 copy-start.20
  33.8 0.7 copy-start.23
  34.5 14.7 %copy-start.8 = (bf16[512,512]{1,0:T(8,128)(2,1)S(1)}, bf16[512,512]{1,0:T(8,128)(2,1)}, u32[]{:S(2)}) copy-start(bf16[512,512]{1,0:T(8,128)(2,1)} %nodes_ref.5) | copy-start | bytes 1572868
  44.8 1.7 %copy-start.30 = (bf16[3072,512]{1,0:T(8,128)(2,1)}, bf16[3072,512]{1,0:T(8,128)(2,1)S(1)}, u32[]{:S(2)}) copy-start(bf16[3072,512]{1,0:T(8,128)(2,1)S(1)} %shard_map.166.part_hbm) | copy-start | bytes 9437188
  46.6 0.6 copy-start.12
  47.3 0.6 copy-start.14
  47.9 0.6 copy-start.16
  48.5 0.6 copy-start.18
  49.2 1.0 copy-start.9
  50.2 1.0 copy-start.10
  51.3 1.0 copy-start.11
  52.3 0.9 copy-start.13
  53.2 0.9 copy-start.15
  54.1 0.9 copy-start.17
  55.0 0.9 copy-start.19
  55.9 0.7 copy-start.21
  56.6 0.7 copy-start.24
  57.3 0.7 copy-start.26
  57.9 0.7 copy-start.27
  58.6 0.7 copy-start.28
  59.3 54.2 %copy-start.1 = (bf16[1536,512]{1,0:T(8,128)(2,1)S(1)}, bf16[1536,512]{1,0:T(8,128)(2,1)}, u32[]{:S(2)}) copy-start(bf16[1536,512]{1,0:T(8,128)(2,1)} %w1_ref.3) | copy-start | bytes 4718596
  95.6 1.0 copy-start.31
  96.5 13.7 %collective-permute-start.6 = (bf16[80,512]{1,0:T(8,128)(2,1)}, bf16[80,512]{1,0:T(8,128)(2,1)S(1)}, u32[]{:S(2)}, u32[]{:S(2)}) collective-permute-start(bf16[80,512]{1,0:T(8,128)(2,1)} %get-tuple-element.37), channel_id=1, source_target_pairs={{0,127},{1,0},{2,1},{3,2},{4,3},{5,4},{6,5},{7,6},{8,7},{9,8},{10,... | collective-permute-start | bytes 245768 | tf_op jit(solution)/shard_map/ppermute | solution.py:26
  96.9 33.0 %collective-permute-start.7 = (bf16[80,512]{1,0:T(8,128)(2,1)}, bf16[80,512]{1,0:T(8,128)(2,1)S(1)}, u32[]{:S(2)}, u32[]{:S(2)}) collective-permute-start(bf16[80,512]{1,0:T(8,128)(2,1)} %get-tuple-element.38), channel_id=1, source_target_pairs={{0,126},{1,127},{2,0},{3,1},{4,2},{5,3},{6,4},{7,5},{8,6},{9,7},{1... | collective-permute-start | bytes 245768 | tf_op jit(solution)/shard_map/ppermute | solution.py:26
  97.7 32.2 %collective-permute-start.8 = (bf16[80,512]{1,0:T(8,128)(2,1)}, bf16[80,512]{1,0:T(8,128)(2,1)S(1)}, u32[]{:S(2)}, u32[]{:S(2)}) collective-permute-start(bf16[80,512]{1,0:T(8,128)(2,1)} %get-tuple-element.39), channel_id=1, source_target_pairs={{0,125},{1,126},{2,127},{3,0},{4,1},{5,2},{6,3},{7,4},{8,5},{9,6},... | collective-permute-start | bytes 245768 | tf_op jit(solution)/shard_map/ppermute | solution.py:26
  98.1 31.9 %collective-permute-start.9 = (bf16[80,512]{1,0:T(8,128)(2,1)S(1)}, bf16[80,512]{1,0:T(8,128)(2,1)S(1)}, u32[]{:S(2)}, u32[]{:S(2)}) collective-permute-start(bf16[80,512]{1,0:T(8,128)(2,1)S(1)} %get-tuple-element.40), channel_id=1, source_target_pairs={{0,1},{1,2},{2,3},{3,4},{4,5},{5,6},{6,7},{7,8},{8,9},{9,10},{10,1... | collective-permute-start | bytes 245768 | tf_op jit(solution)/shard_map/ppermute | solution.py:26
  99.1 30.9 %collective-permute-start.10 = (bf16[80,512]{1,0:T(8,128)(2,1)S(1)}, bf16[80,512]{1,0:T(8,128)(2,1)S(1)}, u32[]{:S(2)}, u32[]{:S(2)}) collective-permute-start(bf16[80,512]{1,0:T(8,128)(2,1)S(1)} %get-tuple-element.41), channel_id=1, source_target_pairs={{0,2},{1,3},{2,4},{3,5},{4,6},{5,7},{6,8},{7,9},{8,10},{9,11},{10,... | collective-permute-start | bytes 245768 | tf_op jit(solution)/shard_map/ppermute | solution.py:26
  101.5 27.4 %all-to-all-start.1 = ((bf16[128,2,512]{2,1,0:T(2,128)(2,1)}), bf16[128,2,512]{2,1,0:T(2,128)(2,1)}, u32[]{:S(2)}, u32[]{:S(2)}) async-start(bf16[128,2,512]{2,1,0:T(2,128)(2,1)} %all_to_all.17), calls=%async_computation.1 | async-start | bytes 524288 | tf_op jit(solution)/shard_map/all_to_all | solution.py:30
  110.2 19.7 %collective-permute-start.11 = (bf16[80,512]{1,0:T(8,128)(2,1)S(1)}, bf16[80,512]{1,0:T(8,128)(2,1)S(1)}, u32[]{:S(2)}, u32[]{:S(2)}) collective-permute-start(bf16[80,512]{1,0:T(8,128)(2,1)S(1)} %get-tuple-element.42), channel_id=1, source_target_pairs={{0,3},{1,4},{2,5},{3,6},{4,7},{5,8},{6,9},{7,10},{8,11},{9,12},{10... | collective-permute-start | bytes 245768 | tf_op jit(solution)/shard_map/ppermute | solution.py:26
  113.4 1.9 %copy-start.5 = (bf16[3072,512]{1,0:T(8,128)(2,1)S(1)}, bf16[3072,512]{1,0:T(8,128)(2,1)}, u32[]{:S(2)}) copy-start(bf16[3072,512]{1,0:T(8,128)(2,1)} %cot_hbm.3) | copy-start | bytes 9437188
  115.3 0.7 copy-start.22
  116.0 0.7 copy-start.25
  116.8 1.9 %copy-start.29 = (bf16[3072,512]{1,0:T(8,128)(2,1)S(1)}, bf16[3072,512]{1,0:T(8,128)(2,1)}, u32[]{:S(2)}) copy-start(bf16[3072,512]{1,0:T(8,128)(2,1)} %get-tuple-element.34.hgrad_hbm) | copy-start | bytes 9437188
  118.6 1.2 copy-start.32
  119.9 10.1 %copy-start.3 = (s32[1,736]{1,0:T(1,128)S(1)}, s32[1,736]{1,0:T(1,128)}, u32[]{:S(2)}) copy-start(s32[1,736]{1,0:T(1,128)} %list_ref.3) | copy-start | bytes 8836
where the time goes:
time: 133 us; the launch traced here: 131 us
  Pallas kernels  57.5 us (43%)
  starting transfers between devices  41 us (31%)
  local copies, waits for them, and re-layouts  31.9 us (24%)
    pallas_call x1, Pallas kernels, on_device(): kernel_call(main_kernel, [big, sds((count, width), BF), big] + near_shape...  36.3 us
    unnamed x66, local copies, waits for them, and re-layouts  29.2 us
    ppermute x12, starting transfers between devices, shifted(): lax.ppermute(value, AXES, [(s, (s + steps) % count) for s in range(count)])  26.7 us
    all_to_all x2, starting transfers between devices, exchange_far(): return lax.all_to_all(rows, AXES, split_axis=0, concat_axis=0, tiled=True)  14.3 us
    pallas_call x1, Pallas kernels, on_device(): kernel_call(local_kernel, big, [v, v, v, v, a], a, [wide, wide, lanes, la...  10.3 us
    pallas_call x1, Pallas kernels, on_device(): kernel_call(rest_kernel, [big, sds((count, width), F32)], [v] * 4 + [a, a...  8.97 us
    all_to_all x4, local copies, waits for them, and re-layouts, exchange_far(): return lax.all_to_all(rows, AXES, split_axis=0, concat_axis=0, tiled=True)  2.76 us
  transfers between devices with their start and end apart: 14, of which 0 were waited for; matrix products, arithmetic and copies ran while one was open for 0% of the time, Pallas kernels for 15%

commit v1 on v0

v1 whole, which is shorter than its diff:
```python
import functools

import jax
import jax.numpy as jnp
from jax import lax
from jax.experimental import pallas as pl
from jax.experimental.pallas import tpu as pltpu
from jax.sharding import PartitionSpec as P

NEAR = 80
NEAR_TOTAL = 480
TILE = 256
BF = jnp.bfloat16
F32 = jnp.float32
AXES = ("region", "sub")
VMEM = pltpu.VMEM
MIB = 1024 * 1024
I16 = jnp.int16
VMEM_LIMIT = 60 * MIB
STEP_LOCAL = 1024
STEP_MAIN = 1024
STEP_REST = 1536


def near_offset(neighbour):
    return neighbour + 1 if neighbour < 3 else 2 - neighbour


def shifted(value, steps):
    count = lax.axis_size(AXES)
    return lax.ppermute(value, AXES, [(s, (s + steps) % count) for s in range(count)])


def exchange_far(rows):
    return lax.all_to_all(rows, AXES, split_axis=0, concat_axis=0, tiled=True)


def dot(a, b):
    return lax.dot_general(a, b, (((1,), (0,)), ((), ())), preferred_element_type=F32)


def dot_nt(a, b):
    return lax.dot_general(a, b, (((1,), (1,)), ((), ())), preferred_element_type=F32)


def dot_tn(a, b):
    return lax.dot_general(a, b, (((0,), (0,)), ((), ())), preferred_element_type=F32)


def hot_rows(index_row, first, count):
    n = index_row.shape[1]
    block = jnp.broadcast_to(index_row - first, (16, n)).astype(I16)
    ids = lax.broadcasted_iota(jnp.int32, (16, n), 0).astype(I16)
    one, zero = jnp.ones((16, n), BF), jnp.zeros((16, n), BF)
    return jnp.concatenate(
        [jnp.where(block == ids + I16(16 * k), one, zero) for k in range(count // 16)], axis=0
    )


def hot_columns(index_lanes, first, count):
    lane = lax.broadcasted_iota(jnp.int32, index_lanes.shape, 1).astype(I16)
    one, zero = jnp.ones(index_lanes.shape, BF), jnp.zeros(index_lanes.shape, BF)
    parts = [
        jnp.where(index_lanes == lane + I16(128 * k + first), one, zero) for k in range(count // 128)
    ]
    return jnp.concatenate(parts, axis=1)


def spread_lanes(index, lanes_ref):
    flipped = jnp.transpose(index, (1, 0))
    for j in range(index.shape[0]):
        lanes_ref[pl.ds(j * 128, 128), :] = jnp.broadcast_to(flipped[:, j : j + 1], (128, 128)).astype(I16)


def index_row(ref, t, step):
    per = step // 128
    return jnp.concatenate([ref[pl.ds(t * per + i, 1), :] for i in range(per)], axis=1)


def row_mean(x):
    return jnp.sum(x, axis=1, keepdims=True) * (1.0 / x.shape[1])


def normalise(mixed):
    centre = mixed - row_mean(mixed)
    spread = lax.rsqrt(row_mean(centre * centre) + 1e-05)
    return centre * spread, spread


def norm_back(scaled, normal, spread):
    return spread * (scaled - row_mean(scaled) - normal * row_mean(scaled * normal))


def silu_parts(x):
    sigma = 0.5 * jnp.tanh(0.5 * x) + 0.5
    active = x * sigma
    return active, sigma + active * (1.0 - sigma)


def step_rows(t, step):
    return pl.ds(pl.multiple_of(t * step, step), step)


def piece(t, step, src, dst, sems):
    rows = step_rows(t, step)
    return pltpu.make_async_copy(src.at[rows], dst.at[rows], sems.at[t])


def live_rows(counts_ref, t, step):
    position = lax.broadcasted_iota(jnp.int32, (step, 1), 0)
    tiles = step // TILE
    limit = counts_ref[t * tiles]
    for i in range(1, tiles):
        limit = jnp.where(position >= i * TILE, counts_ref[t * tiles + i] + i * TILE, limit)
    return position < limit


def fetch(sems, *pairs):
    copies = [pltpu.make_async_copy(s, d, sems.at[i]) for i, (s, d) in enumerate(pairs)]
    for c in copies:
        c.start()
    return copies


def gather_kernel(nodes_hbm, list_hbm, *refs):
    outs, (nodes, slots, sems) = refs[:7], refs[7:]
    for c in fetch(sems, (list_hbm, slots), (nodes_hbm, nodes)):
        c.wait()
    hot = hot_rows(slots[...], 0, nodes.shape[0])
    rows = dot_tn(hot, nodes[...]).astype(BF)
    for i in range(6):
        outs[i][...] = rows[i * NEAR : (i + 1) * NEAR]
    outs[6][...] = rows[NEAR_TOTAL:]


def local_kernel(
    nodes_hbm, sender_hbm, receiver_hbm, w1_hbm, edges_hbm, part_hbm,
    nodes, sender, receiver, w1, edges, part, slanes, rlanes, table, sems, in_sem, out_sem,
):
    step = STEP_LOCAL
    steps = edges.shape[0] // step
    count, width = nodes.shape
    first = fetch(sems, (sender_hbm, sender), (receiver_hbm, receiver), (nodes_hbm, nodes), (w1_hbm, w1))
    for t in range(steps):
        piece(t, step, edges_hbm, edges, in_sem).start()
    for c in first[:2]:
        c.wait()
    spread_lanes(sender[...], slanes)
    spread_lanes(receiver[...], rlanes)
    for c in first[2:]:
        c.wait()
    table[:count, :] = dot(nodes[...], w1[width : 2 * width, :]).astype(BF)
    table[count:, :] = dot(nodes[...], w1[2 * width :, :]).astype(BF)

    def body(t, carry):
        rows = step_rows(t, step)
        piece(t, step, edges_hbm, edges, in_sem).wait()
        hot = jnp.concatenate(
            [hot_columns(slanes[rows, :], 0, count), hot_columns(rlanes[rows, :], 0, count)], axis=1
        )
        total = dot(hot, table[...]) + dot(edges[rows, :], w1[:width, :])
        part[rows, :] = total.astype(BF)
        piece(t, step, part, part_hbm, out_sem).start()
        return carry

    lax.fori_loop(0, steps, body, 0)
    for t in range(steps):
        piece(t, step, part, part_hbm, out_sem).wait()


def main_kernel(
    counts_ref, n0, n1, n2, n3, n4, n5, far_hbm, sender_hbm, receiver_hbm,
    w1_hbm, w2_hbm, gain_hbm, nw1_hbm, nw2_hbm, ngain_hbm, nodes_hbm, ncot_hbm,
    part_hbm, edges_hbm, cot_hbm,
    edge_out_hbm, node_out_hbm, hgrad_hbm, r0, r1, r2, r3, r4, r5, rfar, direct_hbm,
    arrived, sender, receiver, w1s, w2, gain_ref, nw1, nw2, ngain, nodes, ncot,
    part, edges, cot, eout, normals, slopes, hgrad, slanes, rlanes, spreads, table, sums, aggregate,
    agrad, node_out, direct, w2t,
    sems, node_sem, part_sem, edges_sem, cot_sem, eout_sem, hgrad_sem, last_sem,
):
    step = STEP_MAIN
    steps = edges.shape[0] // step
    count, width = nodes.shape
    halo = table.shape[0]
    fed = arrived.shape[0]
    near = [(n, arrived.at[pl.ds(i * NEAR, NEAR)]) for i, n in enumerate((n0, n1, n2, n3, n4, n5))]
    first = fetch(
        sems, (sender_hbm, sender), (receiver_hbm, receiver), (w1_hbm.at[pl.ds(width, width)], w1s), *near,
        (far_hbm, arrived.at[pl.ds(NEAR_TOTAL, fed - NEAR_TOTAL)]),
        (w2_hbm, w2), (gain_hbm, gain_ref),
    )
    for t in range(steps):
        piece(t, step, part_hbm, part, part_sem).start()
    for t in range(steps):
        piece(t, step, edges_hbm, edges, edges_sem).start()
    later = fetch(
        node_sem, (nw1_hbm, nw1), (nw2_hbm, nw2), (ngain_hbm, ngain), (nodes_hbm, nodes), (ncot_hbm, ncot),
    )
    for t in range(steps):
        piece(t, step, cot_hbm, cot, cot_sem).start()
    for c in first[:2]:
        c.wait()
    spread_lanes(sender[...], slanes)
    spread_lanes(receiver[...], rlanes)
    aggregate[...] = jnp.zeros_like(aggregate)
    sums[...] = jnp.zeros_like(sums)
    for c in first[2:]:
        c.wait()
    table[:fed, :] = dot(arrived[...], w1s[...]).astype(BF)
    table[fed:, :] = jnp.zeros((halo - fed, width), BF)
    gain = gain_ref[...]

    def forward(t, carry):
        rows = step_rows(t, step)
        piece(t, step, part_hbm, part, part_sem).wait()
        hot = hot_columns(slanes[rows, :], count, halo)
        hidden = part[rows, :].astype(F32) + dot(hot, table[...])
        active, slope = silu_parts(hidden)
        slopes[rows, :] = slope.astype(BF)
        normal, spread = normalise(dot(active.astype(BF), w2[...]))
        normals[rows, :] = normal.astype(BF)
        spreads[rows, :] = spread
        message = jnp.where(live_rows(counts_ref, t, step), normal * gain, 0.0)
        piece(t, step, edges_hbm, edges, edges_sem).wait()
        eout[rows, :] = (edges[rows, :].astype(F32) + message).astype(BF)
        into = hot_rows(index_row(receiver, t, step), 0, count)
        aggregate[...] += dot(into, message.astype(BF))
        piece(t, step, eout, edge_out_hbm, eout_sem).start()
        return carry

    lax.fori_loop(0, steps, forward, 0)
    for c in later:
        c.wait()

    node_hidden = dot(nodes[...], nw1[:width, :]) + dot(aggregate[...].astype(BF), nw1[width:, :])
    active, node_slope = silu_parts(node_hidden)
    node_mixed = dot(active.astype(BF), nw2[...])
    normal, spread = normalise(node_mixed)
    node_out[...] = (nodes[...].astype(F32) + normal * ngain[...]).astype(BF)
    node_cot = ncot[...].astype(F32)
    mixed_grad = norm_back(node_cot * ngain[...], normal, spread).astype(BF)
    hidden_grad = (dot_nt(mixed_grad, nw2[...]) * node_slope).astype(BF)
    direct[...] = node_cot + dot_nt(hidden_grad, nw1[:width, :])
    agrad[...] = dot_nt(hidden_grad, nw1[width:, :]).astype(BF)
    ends = fetch(last_sem, (node_out, node_out_hbm), (direct, direct_hbm))
    w2t[...] = jnp.transpose(w2[...], (1, 0))

    def backward(t, carry):
        rows = step_rows(t, step)
        upper = dot(hot_columns(rlanes[rows, :], 0, count), agrad[...])
        piece(t, step, cot_hbm, cot, cot_sem).wait()
        live = live_rows(counts_ref, t, step)
        scaled = jnp.where(live, (upper + cot[rows, :].astype(F32)) * gain, 0.0)
        grad = norm_back(scaled, normals[rows, :].astype(F32), spreads[rows, :]).astype(BF)
        hg = (dot(grad, w2t[...]) * slopes[rows, :].astype(F32)).astype(BF)
        hgrad[rows, :] = hg
        sums[...] += dot(hot_rows(index_row(sender, t, step), count, halo), hg)
        piece(t, step, hgrad, hgrad_hbm, hgrad_sem).start()
        return carry

    lax.fori_loop(0, steps, backward, 0)
    back = dot_nt(sums[...].astype(BF), w1s[...]).astype(BF)
    for i, ref in enumerate((r0, r1, r2, r3, r4, r5)):
        ref[...] = back[i * NEAR : (i + 1) * NEAR]
    rfar[...] = back[NEAR_TOTAL:fed]
    for t in range(steps):
        piece(t, step, eout, edge_out_hbm, eout_sem).wait()
        piece(t, step, hgrad, hgrad_hbm, hgrad_sem).wait()
    for c in ends:
        c.wait()


def rest_kernel(
    sender_hbm, receiver_hbm, w1_hbm, direct_hbm, hgrad_hbm, cot_hbm, grad_hbm, owned_hbm,
    sender, receiver, w1, direct, hgrad, cot, sums, w1t, sems, h_sem, c_sem, out_sem, last_sem,
):
    step = STEP_REST
    steps = hgrad.shape[0] // step
    count, width = direct.shape
    first = fetch(sems, (sender_hbm, sender), (receiver_hbm, receiver), (w1_hbm, w1), (direct_hbm, direct))
    for t in range(steps):
        piece(t, step, hgrad_hbm, hgrad, h_sem).start()
        piece(t, step, cot_hbm, cot, c_sem).start()
    sums[...] = jnp.zeros_like(sums)
    for c in first:
        c.wait()
    w1t[...] = jnp.transpose(w1[:width, :], (1, 0))

    def body(t, carry):
        rows = step_rows(t, step)
        piece(t, step, hgrad_hbm, hgrad, h_sem).wait()
        piece(t, step, cot_hbm, cot, c_sem).wait()
        hg = hgrad[rows, :]
        cot[rows, :] = (cot[rows, :].astype(F32) + dot(hg, w1t[...])).astype(BF)
        hot = jnp.concatenate(
            [hot_rows(index_row(sender, t, step), 0, count), hot_rows(index_row(receiver, t, step), 0, count)],
            axis=0,
        )
        sums[...] += dot(hot, hg)
        piece(t, step, cot, grad_hbm, out_sem).start()
        return carry

    lax.fori_loop(0, steps, body, 0)
    direct[...] = (
        direct[...]
        + dot_nt(sums[:count, :].astype(BF), w1[width : 2 * width, :])
        + dot_nt(sums[count:, :].astype(BF), w1[2 * width :, :])
    )
    for c in fetch(last_sem, (direct, owned_hbm)):
        c.wait()
    for t in range(steps):
        piece(t, step, cot, grad_hbm, out_sem).wait()


def final_kernel(
    list_hbm, owned_hbm, n0, n1, n2, n3, n4, n5, far_hbm, out_hbm,
    slots, owned, returned, out, sems, last_sem,
):
    fed = returned.shape[0]
    near = [(n, returned.at[pl.ds(i * NEAR, NEAR)]) for i, n in enumerate((n0, n1, n2, n3, n4, n5))]
    for c in fetch(
        sems, (list_hbm, slots), (owned_hbm, owned), *near,
        (far_hbm, returned.at[pl.ds(NEAR_TOTAL, fed - NEAR_TOTAL)]),
    ):
        c.wait()
    hot = hot_rows(slots[...], 0, owned.shape[0])
    out[...] = (owned[...] + dot(hot, returned[...])).astype(BF)
    for c in fetch(last_sem, (out, out_hbm)):
        c.wait()


def kernel_call(body, outs, in_specs, out_specs, scratch, flops, moved):
    return pl.pallas_call(
        body,
        out_shape=outs,
        in_specs=in_specs,
        out_specs=out_specs,
        scratch_shapes=scratch,
        compiler_params=pltpu.CompilerParams(vmem_limit_bytes=VMEM_LIMIT),
        cost_estimate=pl.CostEstimate(flops=flops, bytes_accessed=moved, transcendentals=0),
    )


def on_device(
    nodes, edges, sender, receiver, tile_counts, send_list, edge_w1, edge_w2, edge_gain,
    node_w1, node_w2, node_gain, node_cotangent, edge_cotangent,
):
    count, width = nodes.shape
    slots = edges.shape[0]
    halo = send_list.shape[1]
    far_rows = halo - NEAR_TOTAL
    padded = -(-halo // 256) * 256
    v = pl.BlockSpec(memory_space=pltpu.VMEM)
    s = pl.BlockSpec(memory_space=pltpu.SMEM)
    a = pl.BlockSpec(memory_space=pl.ANY)
    sds = jax.ShapeDtypeStruct
    sem = lambda n: pltpu.SemaphoreType.DMA((n,))
    near_shapes = [sds((NEAR, width), BF)] * 6 + [sds((far_rows, width), BF)]
    big = sds((slots, width), BF)
    wide = VMEM((slots, width), BF)
    lanes = VMEM((slots, 128), I16)
    index = VMEM((slots // 128, 128), jnp.int32)
    listed = VMEM((1, halo), jnp.int32)
    block = VMEM((count, width), BF)
    block32 = VMEM((count, width), F32)
    mat = VMEM((width, width), BF)
    vec = VMEM((1, width), F32)
    w1 = VMEM((3 * width, width), BF)
    square = 2 * count * width * width

    sender = sender.reshape(slots // 128, 128)
    receiver = receiver.reshape(slots // 128, 128)
    gain = edge_gain.reshape(1, width)
    ngain = node_gain.reshape(1, width)

    leaving = kernel_call(
        gather_kernel, near_shapes, [a, a], [v] * 7, [block, listed, sem(2)],
        2 * halo * count * width, 2 * MIB,
    )(nodes, send_list)
    arrived = [shifted(leaving[i], near_offset(i)) for i in range(6)]
    far = exchange_far(leaving[6])

    n = slots // STEP_LOCAL
    part = kernel_call(
        local_kernel, big, [a] * 5, a,
        [block, index, index, w1, wide, wide, lanes, lanes, VMEM((2 * count, width), BF), sem(4), sem(n), sem(n)],
        20 * square, 8 * MIB,
    )(nodes, sender, receiver, edge_w1, edges)

    n = slots // STEP_MAIN
    outs = kernel_call(
        main_kernel,
        [big, sds((count, width), BF), big] + near_shapes + [sds((count, width), F32)],
        [s] + [a] * 20,
        [a, a, a] + [v] * 7 + [a],
        [VMEM((halo, width), BF), index, index, mat, mat, vec, VMEM((2 * width, width), BF), mat, vec, block, block]
        + [wide] * 7
        + [lanes, lanes, VMEM((slots, 1), F32), VMEM((padded, width), BF), VMEM((padded, width), F32),
           block32, block, block, block32, mat]
        + [sem(12), sem(5)] + [sem(n)] * 5 + [sem(2)],
        50 * square, 20 * MIB,
    )(
        tile_counts, *arrived, far, sender, receiver, edge_w1, edge_w2, gain, node_w1, node_w2, ngain,
        nodes, node_cotangent, part, edges, edge_cotangent,
    )
    edge_out, node_out, hgrad = outs[:3]
    back = outs[3:10]
    direct = outs[10]
    returned = [shifted(back[i], -near_offset(i)) for i in range(6)]
    far_back = exchange_far(back[6])

    n = slots // STEP_REST
    grad_edges, owned = kernel_call(
        rest_kernel, [big, sds((count, width), F32)], [a] * 6, [a, a],
        [index, index, w1, block32, wide, wide, VMEM((2 * count, width), F32), mat, sem(4), sem(n), sem(n), sem(n), sem(1)],
        20 * square, 12 * MIB,
    )(sender, receiver, edge_w1, direct, hgrad, edge_cotangent)

    grad_nodes = kernel_call(
        final_kernel, sds((count, width), BF), [a] * 9, a,
        [listed, block32, VMEM((halo, width), BF), block, sem(9), sem(1)], 2 * square, 3 * MIB,
    )(send_list, owned, *returned, far_back)
    return edge_out, node_out, grad_edges, grad_nodes


def solution(mesh):
    rows = P(AXES, None)
    flat = P(AXES)
    in_specs = (
        rows, rows, flat, flat, flat, rows, P(), P(), P(), P(), P(), P(), rows, rows,
    )
    return jax.shard_map(
        on_device, mesh=mesh, in_specs=in_specs, out_specs=(rows,) * 4, check_vma=False
    )
```

time: 133 us -> 103 us (0.77)
  local copies, waits for them, and re-layouts: 31.9 us -> 6.49 us
  Pallas kernels: 57.5 us -> 54.2 us
    unnamed x66 -> x24, local copies, waits for them, and re-layouts: 29.2 us -> 1.37 us
    pallas_call x1, Pallas kernels: 36.3 us -> 29.5 us  [on_device(): kernel_call(main_kernel, [big, sds((count, width), BF), big] + near_shape...]
    pallas_call x4, Pallas kernels: 21.2 us -> 24.7 us  [the longest x1 9.95 us: on_device(): kernel_call(rest_kernel, [big, sds((count, width), F32)], [a] * 6, [a, a]...]
    all_to_all x4, local copies, waits for them, and re-layouts: 2.76 us -> 5.11 us  [exchange_far(): return lax.all_to_all(rows, AXES, split_axis=0, concat_axis=0, tiled=True)]
  transfers between devices with their start and end apart: 14 -> 14, of which waited for: 0 -> 0; matrix products, arithmetic and copies ran while one was open for 0% -> 0% of each run, Pallas kernels for 15% -> 19%
where the time goes in v1:
time: 103 us; the launch traced here: 102 us
  Pallas kernels  54.2 us (53%)
  starting transfers between devices  40.7 us (40%)
  local copies, waits for them, and re-layouts  6.49 us (6%)
  between operations  1.05 us (1%)
    pallas_call x1, Pallas kernels, on_device(): kernel_call(main_kernel, [big, sds((count, width), BF), big] + near_shape...  29.5 us
    ppermute x12, starting transfers between devices, shifted(): lax.ppermute(value, AXES, [(s, (s + steps) % count) for s in range(count)])  26.8 us
    all_to_all x2, starting transfers between devices, exchange_far(): return lax.all_to_all(rows, AXES, split_axis=0, concat_axis=0, tiled=True)  13.8 us
    pallas_call x1, Pallas kernels, on_device(): kernel_call(rest_kernel, [big, sds((count, width), F32)], [a] * 6, [a, a]...  9.95 us
    pallas_call x1, Pallas kernels, on_device(): kernel_call(local_kernel, big, [a] * 5, a, [block, index, index, w1, wide...  9.53 us
    all_to_all x4, local copies, waits for them, and re-layouts, exchange_far(): return lax.all_to_all(rows, AXES, split_axis=0, concat_axis=0, tiled=True)  5.11 us
    pallas_call x1, Pallas kernels, on_device(): kernel_call(final_kernel, sds((count, width), BF), [a] * 9, a, [listed, b...  2.88 us
    pallas_call x1, Pallas kernels, on_device(): kernel_call(gather_kernel, near_shapes, [a, a], [v] * 7, [block, listed,...  2.37 us
  transfers between devices with their start and end apart: 14, of which 0 were waited for; matrix products, arithmetic and copies ran while one was open for 0% of the time, Pallas kernels for 19%

profile of v1, /device:TPU:1, one launch (start us, length us, event | category | flops | bytes accessed | tf_op | source)
XLA Modules:
  0.0 102.5 jit_solution(11479654963714507511)
XLA Ops:
  0.6 2.4 %shard_map.165 = (bf16[80,512]{1,0:T(8,128)(2,1)}, bf16[80,512]{1,0:T(8,128)(2,1)}, bf16[80,512]{1,0:T(8,128)(2,1)}, bf16[80,512]{1,0:T(8,128)(2,1)}, bf16[80,51...) custom-call(bf16[512,512]{1,0:T(8,128)(2,1)} %nodes_hbm.5, s32[1,736]{1,0:T(1,128)} %list_hbm.3), custom_call_target="tpu_custom_call" | custom-call | flops 385875968 | bytes 2097152 | tf_op jit(solution)/shard_map/pallas_call | solution.py:376
  3.0 2.8 %collective-permute-start = (bf16[80,512]{1,0:T(8,128)(2,1)}, bf16[80,512]{1,0:T(8,128)(2,1)S(1)}, u32[]{:S(2)}, u32[]{:S(2)}) collective-permute-start(bf16[80,512]{1,0:T(8,128)(2,1)} %get-tuple-element.24), channel_id=1, source_target_pairs={{0,1},{1,2},{2,3},{3,4},{4,5},{5,6},{6,7},{7,8},{8,9},{9,10},{10,1... | collective-permute-start | bytes 245768 | tf_op jit(solution)/shard_map/ppermute | solution.py:31
  5.8 1.3 %collective-permute-start.1 = (bf16[80,512]{1,0:T(8,128)(2,1)}, bf16[80,512]{1,0:T(8,128)(2,1)S(1)}, u32[]{:S(2)}, u32[]{:S(2)}) collective-permute-start(bf16[80,512]{1,0:T(8,128)(2,1)} %get-tuple-element.25), channel_id=1, source_target_pairs={{0,2},{1,3},{2,4},{3,5},{4,6},{5,7},{6,8},{7,9},{8,10},{9,11},{10,... | collective-permute-start | bytes 245768 | tf_op jit(solution)/shard_map/ppermute | solution.py:31
  7.1 1.7 %collective-permute-start.2 = (bf16[80,512]{1,0:T(8,128)(2,1)}, bf16[80,512]{1,0:T(8,128)(2,1)S(1)}, u32[]{:S(2)}, u32[]{:S(2)}) collective-permute-start(bf16[80,512]{1,0:T(8,128)(2,1)} %get-tuple-element.26), channel_id=1, source_target_pairs={{0,3},{1,4},{2,5},{3,6},{4,7},{5,8},{6,9},{7,10},{8,11},{9,12},{10... | collective-permute-start | bytes 245768 | tf_op jit(solution)/shard_map/ppermute | solution.py:31
  8.7 0.0 collective-permute-start.3
  8.8 5.6 %collective-permute-start.4 = (bf16[80,512]{1,0:T(8,128)(2,1)}, bf16[80,512]{1,0:T(8,128)(2,1)S(1)}, u32[]{:S(2)}, u32[]{:S(2)}) collective-permute-start(bf16[80,512]{1,0:T(8,128)(2,1)} %get-tuple-element.28), channel_id=1, source_target_pairs={{0,126},{1,127},{2,0},{3,1},{4,2},{5,3},{6,4},{7,5},{8,6},{9,7},{1... | collective-permute-start | bytes 245768 | tf_op jit(solution)/shard_map/ppermute | solution.py:31
  14.4 1.8 %all_to_all.14 = bf16[128,2,512]{2,1,0:T(2,128)(2,1)} reshape(bf16[256,512]{1,0:T(8,128)(2,1)} %get-tuple-element.30) | data formatting | bytes 524288 | tf_op jit(solution)/shard_map/all_to_all | solution.py:35
  16.1 5.6 %all-to-all-start = ((bf16[128,2,512]{2,1,0:T(2,128)(2,1)}), bf16[128,2,512]{2,1,0:T(2,128)(2,1)S(1)}, u32[]{:S(2)}, u32[]{:S(2)}) async-start(bf16[128,2,512]{2,1,0:T(2,128)(2,1)} %all_to_all.14), calls=%async_computation | async-start | bytes 524288 | tf_op jit(solution)/shard_map/all_to_all | solution.py:35
  21.7 0.0 collective-permute-done.n0
  21.7 0.0 copy-start.6
  21.7 8.0 %collective-permute-start.5 = (bf16[80,512]{1,0:T(8,128)(2,1)}, bf16[80,512]{1,0:T(8,128)(2,1)S(1)}, u32[]{:S(2)}, u32[]{:S(2)}) collective-permute-start(bf16[80,512]{1,0:T(8,128)(2,1)} %get-tuple-element.29), channel_id=1, source_target_pairs={{0,125},{1,126},{2,127},{3,0},{4,1},{5,2},{6,3},{7,4},{8,5},{9,6},... | collective-permute-start | bytes 245768 | tf_op jit(solution)/shard_map/ppermute | solution.py:31
  29.8 9.5 %shard_map.166.part_hbm = bf16[3072,512]{1,0:T(8,128)(2,1)} custom-call(bf16[512,512]{1,0:T(8,128)(2,1)} %nodes_hbm.5, s32[24,128]{1,0:T(8,128)} %bitcast.4, s32[24,128]{1,0:T(8,128)} %bitcast.7, bf16[1536,512]{1,0:T(8,128)(2,1)} %w1_hbm.5, bf16[3072,512]{1,0:T(8,128)(2,1)} %edges_hbm.3), custom_call_target="tpu_custom_call" | custom-call | flops 5368709120 | bytes 8388608 | tf_op jit(solution)/shard_map/pallas_call | solution.py:384
  39.3 0.0 copy-done.6
  39.3 0.0 all-to-all-done
  39.3 0.8 all_to_all.16.far_hbm
  40.1 0.0 collective-permute-done.1.n1
  40.1 0.0 copy-start.7
  40.1 0.0 collective-permute-done.2.n2
  40.1 0.0 copy-start.8
  40.1 0.0 collective-permute-done.3.n3
  40.2 0.0 copy-start.9
  40.2 0.0 collective-permute-done.4.n4
  40.2 0.0 copy-start.10
  40.2 0.0 collective-permute-done.5.n5
  40.2 0.0 copy-start.11
  40.2 0.5 copy-done.7
  40.7 0.1 copy-done.8
  40.8 0.0 copy-done.9
  40.8 0.0 copy-done.10
  40.9 0.0 copy-done.11
  40.9 29.5 %shard_map.167 = (bf16[3072,512]{1,0:T(8,128)(2,1)}, bf16[512,512]{1,0:T(8,128)(2,1)}, bf16[3072,512]{1,0:T(8,128)(2,1)}, bf16[80,512]{1,0:T(8,128)(2,1)}, bf16[...) custom-call(s32[12]{0:T(128)} %counts_ref.1, ...), custom_call_target="tpu_custom_call" | custom-call | flops 13421772800 | bytes 20971520 | tf_op jit(solution)/shard_map/pallas_call | solution.py:391
  70.4 0.4 collective-permute-start.6
  70.8 0.8 collective-permute-start.7
  71.7 0.3 collective-permute-start.8
  72.0 1.0 %collective-permute-start.9 = (bf16[80,512]{1,0:T(8,128)(2,1)}, bf16[80,512]{1,0:T(8,128)(2,1)S(1)}, u32[]{:S(2)}, u32[]{:S(2)}) collective-permute-start(bf16[80,512]{1,0:T(8,128)(2,1)} %get-tuple-element.40), channel_id=1, source_target_pairs={{0,1},{1,2},{2,3},{3,4},{4,5},{5,6},{6,7},{7,8},{8,9},{9,10},{10,1... | collective-permute-start | bytes 245768 | tf_op jit(solution)/shard_map/ppermute | solution.py:31
  73.0 1.6 %collective-permute-start.10 = (bf16[80,512]{1,0:T(8,128)(2,1)}, bf16[80,512]{1,0:T(8,128)(2,1)S(1)}, u32[]{:S(2)}, u32[]{:S(2)}) collective-permute-start(bf16[80,512]{1,0:T(8,128)(2,1)} %get-tuple-element.41), channel_id=1, source_target_pairs={{0,2},{1,3},{2,4},{3,5},{4,6},{5,7},{6,8},{7,9},{8,10},{9,11},{10,... | collective-permute-start | bytes 245768 | tf_op jit(solution)/shard_map/ppermute | solution.py:31
  74.6 1.8 %all_to_all.17 = bf16[128,2,512]{2,1,0:T(2,128)(2,1)} reshape(bf16[256,512]{1,0:T(8,128)(2,1)} %get-tuple-element.43) | data formatting | bytes 524288 | tf_op jit(solution)/shard_map/all_to_all | solution.py:35
  76.4 8.3 %all-to-all-start.1 = ((bf16[128,2,512]{2,1,0:T(2,128)(2,1)}), bf16[128,2,512]{2,1,0:T(2,128)(2,1)S(1)}, u32[]{:S(2)}, u32[]{:S(2)}) async-start(bf16[128,2,512]{2,1,0:T(2,128)(2,1)} %all_to_all.17), calls=%async_computation.1 | async-start | bytes 524288 | tf_op jit(solution)/shard_map/all_to_all | solution.py:35
  84.6 0.0 collective-permute-done.6.n0
  84.6 0.0 copy-start
  84.7 3.2 %collective-permute-start.11 = (bf16[80,512]{1,0:T(8,128)(2,1)}, bf16[80,512]{1,0:T(8,128)(2,1)S(1)}, u32[]{:S(2)}, u32[]{:S(2)}) collective-permute-start(bf16[80,512]{1,0:T(8,128)(2,1)} %get-tuple-element.42), channel_id=1, source_target_pairs={{0,3},{1,4},{2,5},{3,6},{4,7},{5,8},{6,9},{7,10},{8,11},{9,12},{10... | collective-permute-start | bytes 245768 | tf_op jit(solution)/shard_map/ppermute | solution.py:31
  87.9 9.9 %shard_map.168 = (bf16[3072,512]{1,0:T(8,128)(2,1)}, f32[512,512]{1,0:T(8,128)}) custom-call(s32[24,128]{1,0:T(8,128)} %bitcast.6, s32[24,128]{1,0:T(8,128)} %bitcast.9, bf16[1536,512]{1,0:T(8,128)(2,1)} %w1_hbm.5, f32[512,512]{1,0:T(8,128)} %get-tuple-element.33.direct_hbm, bf16[3072,512]{1,0:T(8,128)(2,1)} %get-tuple-element.34.hgrad_hbm, ...), custom_call_target="tpu_custom_call" | custom-call | flops 5368709120 | bytes 12582912 | tf_op jit(solution)/shard_map/pallas_call | solution.py:413
  97.8 0.0 copy-done
  97.8 0.0 all-to-all-done.1
  97.8 0.8 all_to_all.19.far_hbm
  98.6 0.0 collective-permute-done.7.n1
  98.7 0.0 copy-start.1
  98.7 0.0 collective-permute-done.8.n2
  98.7 0.0 copy-start.2
  98.7 0.0 collective-permute-done.9.n3
  98.7 0.0 copy-start.3
  98.7 0.0 collective-permute-done.10.n4
  98.7 0.0 copy-start.4
  98.7 0.0 collective-permute-done.11.n5
  98.7 0.0 copy-start.5
  98.7 0.6 copy-done.1
  99.3 0.0 copy-done.2
  99.3 0.0 copy-done.3
  99.4 0.0 copy-done.4
  99.4 0.0 copy-done.5
  99.4 2.9 %shard_map.169 = bf16[512,512]{1,0:T(8,128)(2,1)} custom-call(s32[1,736]{1,0:T(1,128)} %list_hbm.3, f32[512,512]{1,0:T(8,128)} %get-tuple-element.36.owned_hbm, bf16[80,512]{1,0:T(8,128)(2,1)} %copy-done, bf16[80,512]{1,0:T(8,128)(2,1)} %copy-done.1, bf16[80,512]{1,0:T(8,128)(2,1)} %copy-done.2, bf16[80,512]{1,0:T(8,128)(2,1)} %copy-done.3, ...), custom_call_target="tpu_custom_call" | custom-call | flops 536870912 | bytes 3145728 | tf_op jit(solution)/shard_map/pallas_call | solution.py:419
Async XLA Ops:
  3.0 18.7 %collective-permute-start = (bf16[80,512]{1,0:T(8,128)(2,1)}, bf16[80,512]{1,0:T(8,128)(2,1)S(1)}, u32[]{:S(2)}, u32[]{:S(2)}) collective-permute-start(bf16[80,512]{1,0:T(8,128)(2,1)} %get-tuple-element.24), channel_id=1, source_target_pairs={{0,1},{1,2},{2,3},{3,4},{4,5},{5,6},{6,7},{7,8},{8,9},{9,10},{10,1... | collective-permute-start | bytes 245768 | tf_op jit(solution)/shard_map/ppermute | solution.py:31
  5.8 34.4 %collective-permute-start.1 = (bf16[80,512]{1,0:T(8,128)(2,1)}, bf16[80,512]{1,0:T(8,128)(2,1)S(1)}, u32[]{:S(2)}, u32[]{:S(2)}) collective-permute-start(bf16[80,512]{1,0:T(8,128)(2,1)} %get-tuple-element.25), channel_id=1, source_target_pairs={{0,2},{1,3},{2,4},{3,5},{4,6},{5,7},{6,8},{7,9},{8,10},{9,11},{10,... | collective-permute-start | bytes 245768 | tf_op jit(solution)/shard_map/ppermute | solution.py:31
  7.1 33.1 %collective-permute-start.2 = (bf16[80,512]{1,0:T(8,128)(2,1)}, bf16[80,512]{1,0:T(8,128)(2,1)S(1)}, u32[]{:S(2)}, u32[]{:S(2)}) collective-permute-start(bf16[80,512]{1,0:T(8,128)(2,1)} %get-tuple-element.26), channel_id=1, source_target_pairs={{0,3},{1,4},{2,5},{3,6},{4,7},{5,8},{6,9},{7,10},{8,11},{9,12},{10... | collective-permute-start | bytes 245768 | tf_op jit(solution)/shard_map/ppermute | solution.py:31
  8.7 31.4 %collective-permute-start.3 = (bf16[80,512]{1,0:T(8,128)(2,1)}, bf16[80,512]{1,0:T(8,128)(2,1)S(1)}, u32[]{:S(2)}, u32[]{:S(2)}) collective-permute-start(bf16[80,512]{1,0:T(8,128)(2,1)} %get-tuple-element.27), channel_id=1, source_target_pairs={{0,127},{1,0},{2,1},{3,2},{4,3},{5,4},{6,5},{7,6},{8,7},{9,8},{10,... | collective-permute-start | bytes 245768 | tf_op jit(solution)/shard_map/ppermute | solution.py:31
  8.8 31.4 %collective-permute-start.4 = (bf16[80,512]{1,0:T(8,128)(2,1)}, bf16[80,512]{1,0:T(8,128)(2,1)S(1)}, u32[]{:S(2)}, u32[]{:S(2)}) collective-permute-start(bf16[80,512]{1,0:T(8,128)(2,1)} %get-tuple-element.28), channel_id=1, source_target_pairs={{0,126},{1,127},{2,0},{3,1},{4,2},{5,3},{6,4},{7,5},{8,6},{9,7},{1... | collective-permute-start | bytes 245768 | tf_op jit(solution)/shard_map/ppermute | solution.py:31
  16.1 23.2 %all-to-all-start = ((bf16[128,2,512]{2,1,0:T(2,128)(2,1)}), bf16[128,2,512]{2,1,0:T(2,128)(2,1)S(1)}, u32[]{:S(2)}, u32[]{:S(2)}) async-start(bf16[128,2,512]{2,1,0:T(2,128)(2,1)} %all_to_all.14), calls=%async_computation | async-start | bytes 524288 | tf_op jit(solution)/shard_map/all_to_all | solution.py:35
  21.7 17.6 %copy-start.6 = (bf16[80,512]{1,0:T(8,128)(2,1)}, bf16[80,512]{1,0:T(8,128)(2,1)S(1)}, u32[]{:S(2)}) copy-start(bf16[80,512]{1,0:T(8,128)(2,1)S(1)} %collective-permute-done.n0) | copy-start | bytes 245764
  21.7 18.5 %collective-permute-start.5 = (bf16[80,512]{1,0:T(8,128)(2,1)}, bf16[80,512]{1,0:T(8,128)(2,1)S(1)}, u32[]{:S(2)}, u32[]{:S(2)}) collective-permute-start(bf16[80,512]{1,0:T(8,128)(2,1)} %get-tuple-element.29), channel_id=1, source_target_pairs={{0,125},{1,126},{2,127},{3,0},{4,1},{5,2},{6,3},{7,4},{8,5},{9,6},... | collective-permute-start | bytes 245768 | tf_op jit(solution)/shard_map/ppermute | solution.py:31
  40.1 0.6 copy-start.7
  40.1 0.7 copy-start.8
  40.2 0.7 copy-start.9
  40.2 0.7 copy-start.10
  40.2 0.7 copy-start.11
  70.4 14.2 %collective-permute-start.6 = (bf16[80,512]{1,0:T(8,128)(2,1)}, bf16[80,512]{1,0:T(8,128)(2,1)S(1)}, u32[]{:S(2)}, u32[]{:S(2)}) collective-permute-start(bf16[80,512]{1,0:T(8,128)(2,1)} %get-tuple-element.37), channel_id=1, source_target_pairs={{0,127},{1,0},{2,1},{3,2},{4,3},{5,4},{6,5},{7,6},{8,7},{9,8},{10,... | collective-permute-start | bytes 245768 | tf_op jit(solution)/shard_map/ppermute | solution.py:31
  70.8 27.8 %collective-permute-start.7 = (bf16[80,512]{1,0:T(8,128)(2,1)}, bf16[80,512]{1,0:T(8,128)(2,1)S(1)}, u32[]{:S(2)}, u32[]{:S(2)}) collective-permute-start(bf16[80,512]{1,0:T(8,128)(2,1)} %get-tuple-element.38), channel_id=1, source_target_pairs={{0,126},{1,127},{2,0},{3,1},{4,2},{5,3},{6,4},{7,5},{8,6},{9,7},{1... | collective-permute-start | bytes 245768 | tf_op jit(solution)/shard_map/ppermute | solution.py:31
  71.7 27.0 %collective-permute-start.8 = (bf16[80,512]{1,0:T(8,128)(2,1)}, bf16[80,512]{1,0:T(8,128)(2,1)S(1)}, u32[]{:S(2)}, u32[]{:S(2)}) collective-permute-start(bf16[80,512]{1,0:T(8,128)(2,1)} %get-tuple-element.39), channel_id=1, source_target_pairs={{0,125},{1,126},{2,127},{3,0},{4,1},{5,2},{6,3},{7,4},{8,5},{9,6},... | collective-permute-start | bytes 245768 | tf_op jit(solution)/shard_map/ppermute | solution.py:31
  72.0 26.7 %collective-permute-start.9 = (bf16[80,512]{1,0:T(8,128)(2,1)}, bf16[80,512]{1,0:T(8,128)(2,1)S(1)}, u32[]{:S(2)}, u32[]{:S(2)}) collective-permute-start(bf16[80,512]{1,0:T(8,128)(2,1)} %get-tuple-element.40), channel_id=1, source_target_pairs={{0,1},{1,2},{2,3},{3,4},{4,5},{5,6},{6,7},{7,8},{8,9},{9,10},{10,1... | collective-permute-start | bytes 245768 | tf_op jit(solution)/shard_map/ppermute | solution.py:31
  73.0 25.7 %collective-permute-start.10 = (bf16[80,512]{1,0:T(8,128)(2,1)}, bf16[80,512]{1,0:T(8,128)(2,1)S(1)}, u32[]{:S(2)}, u32[]{:S(2)}) collective-permute-start(bf16[80,512]{1,0:T(8,128)(2,1)} %get-tuple-element.41), channel_id=1, source_target_pairs={{0,2},{1,3},{2,4},{3,5},{4,6},{5,7},{6,8},{7,9},{8,10},{9,11},{10,... | collective-permute-start | bytes 245768 | tf_op jit(solution)/shard_map/ppermute | solution.py:31
  76.4 21.5 %all-to-all-start.1 = ((bf16[128,2,512]{2,1,0:T(2,128)(2,1)}), bf16[128,2,512]{2,1,0:T(2,128)(2,1)S(1)}, u32[]{:S(2)}, u32[]{:S(2)}) async-start(bf16[128,2,512]{2,1,0:T(2,128)(2,1)} %all_to_all.17), calls=%async_computation.1 | async-start | bytes 524288 | tf_op jit(solution)/shard_map/all_to_all | solution.py:35
  84.6 13.2 %copy-start = (bf16[80,512]{1,0:T(8,128)(2,1)}, bf16[80,512]{1,0:T(8,128)(2,1)S(1)}, u32[]{:S(2)}) copy-start(bf16[80,512]{1,0:T(8,128)(2,1)S(1)} %collective-permute-done.6.n0) | copy-start | bytes 245764
  84.7 14.1 %collective-permute-start.11 = (bf16[80,512]{1,0:T(8,128)(2,1)}, bf16[80,512]{1,0:T(8,128)(2,1)S(1)}, u32[]{:S(2)}, u32[]{:S(2)}) collective-permute-start(bf16[80,512]{1,0:T(8,128)(2,1)} %get-tuple-element.42), channel_id=1, source_target_pairs={{0,3},{1,4},{2,5},{3,6},{4,7},{5,8},{6,9},{7,10},{8,11},{9,12},{10... | collective-permute-start | bytes 245768 | tf_op jit(solution)/shard_map/ppermute | solution.py:31
  98.7 0.6 copy-start.1
  98.7 0.7 copy-start.2
  98.7 0.7 copy-start.3
  98.7 0.7 copy-start.4
  98.7 0.7 copy-start.5

commit v2 on v1

--- a/solution.py
+++ b/solution.py
@@ -15,8 +15,10 @@
 AXES = ("region", "sub")
 VMEM = pltpu.VMEM
 MIB = 1024 * 1024
+RETURN_ORDER = (3, 4, 5, 0, 1, 2)
 I16 = jnp.int16
 VMEM_LIMIT = 60 * MIB
+SUB = 256
 STEP_LOCAL = 1024
 STEP_MAIN = 1024
 STEP_REST = 1536
@@ -115,6 +117,15 @@
     return position < limit
 
 
+def live_part(counts_ref, t, step, i):
+    position = lax.broadcasted_iota(jnp.int32, (SUB, 1), 0)
+    tile = t * (step // TILE) + i * SUB // TILE
+    limit = counts_ref[tile]
+    for k in range(1, SUB // TILE):
+        limit = jnp.where(position >= k * TILE, counts_ref[tile + k] + k * TILE, limit)
+    return position < limit
+
+
 def fetch(sems, *pairs):
     copies = [pltpu.make_async_copy(s, d, sems.at[i]) for i, (s, d) in enumerate(pairs)]
     for c in copies:
@@ -122,15 +133,32 @@
     return copies
 
 
+def pack_far(rows, wide_ref, out_ref):
+    quarters = rows.shape[1] // 128
+    for c in range(quarters):
+        wide_ref[pl.ds(c, rows.shape[0], stride=quarters), :] = rows[:, c * 128 : (c + 1) * 128]
+    out_ref[...] = wide_ref[...].reshape(out_ref.shape).astype(BF)
+
+
+def unpack_far(packed_ref, wide_ref, out_ref):
+    wide_ref[...] = packed_ref[...].astype(F32).reshape(wide_ref.shape)
+    quarters = out_ref.shape[1] // 128
+    count = wide_ref.shape[0] // quarters
+    for c in range(quarters):
+        out_ref[NEAR_TOTAL:, c * 128 : (c + 1) * 128] = wide_ref[
+            pl.ds(c, count, stride=quarters), :
+        ].astype(BF)
+
+
 def gather_kernel(nodes_hbm, list_hbm, *refs):
-    outs, (nodes, slots, sems) = refs[:7], refs[7:]
+    outs, (nodes, slots, wide, sems) = refs[:7], refs[7:]
     for c in fetch(sems, (list_hbm, slots), (nodes_hbm, nodes)):
         c.wait()
     hot = hot_rows(slots[...], 0, nodes.shape[0])
-    rows = dot_tn(hot, nodes[...]).astype(BF)
+    rows = dot_tn(hot, nodes[...])
     for i in range(6):
-        outs[i][...] = rows[i * NEAR : (i + 1) * NEAR]
-    outs[6][...] = rows[NEAR_TOTAL:]
+        outs[i][...] = rows[i * NEAR : (i + 1) * NEAR].astype(BF)
+    pack_far(rows[NEAR_TOTAL:], wide, outs[6])
 
 
 def local_kernel(
@@ -169,13 +197,13 @@
 
 
 def main_kernel(
-    counts_ref, n0, n1, n2, n3, n4, n5, far_hbm, sender_hbm, receiver_hbm,
+    counts_hbm, n0, n1, n2, n3, n4, n5, far_hbm, sender_hbm, receiver_hbm,
     w1_hbm, w2_hbm, gain_hbm, nw1_hbm, nw2_hbm, ngain_hbm, nodes_hbm, ncot_hbm,
     part_hbm, edges_hbm, cot_hbm,
     edge_out_hbm, node_out_hbm, hgrad_hbm, r0, r1, r2, r3, r4, r5, rfar, direct_hbm,
-    arrived, sender, receiver, w1s, w2, gain_ref, nw1, nw2, ngain, nodes, ncot,
+    counts_ref, far_packed, far_wide, arrived, sender, receiver, w1s, w2, gain_ref, nw1, nw2, ngain, nodes, ncot,
     part, edges, cot, eout, normals, slopes, hgrad, slanes, rlanes, spreads, table, sums, aggregate,
-    agrad, node_out, direct, w2t,
+    agrad, node_out, direct, w2t, w2c, messages,
     sems, node_sem, part_sem, edges_sem, cot_sem, eout_sem, hgrad_sem, last_sem,
 ):
     step = STEP_MAIN
@@ -186,8 +214,7 @@
     near = [(n, arrived.at[pl.ds(i * NEAR, NEAR)]) for i, n in enumerate((n0, n1, n2, n3, n4, n5))]
     first = fetch(
         sems, (sender_hbm, sender), (receiver_hbm, receiver), (w1_hbm.at[pl.ds(width, width)], w1s), *near,
-        (far_hbm, arrived.at[pl.ds(NEAR_TOTAL, fed - NEAR_TOTAL)]),
-        (w2_hbm, w2), (gain_hbm, gain_ref),
+        (far_hbm, far_packed), (counts_hbm, counts_ref), (w2_hbm, w2), (gain_hbm, gain_ref),
     )
     for t in range(steps):
         piece(t, step, part_hbm, part, part_sem).start()
@@ -206,29 +233,51 @@
     sums[...] = jnp.zeros_like(sums)
     for c in first[2:]:
         c.wait()
+    unpack_far(far_packed, far_wide, arrived)
     table[:fed, :] = dot(arrived[...], w1s[...]).astype(BF)
     table[fed:, :] = jnp.zeros((halo - fed, width), BF)
     gain = gain_ref[...]
 
+    w2c[...] = (w2[...].astype(F32) - row_mean(w2[...].astype(F32))).astype(BF)
+    messages[...] = jnp.zeros_like(messages)
+    subs = step // SUB
+
+    def part_of(t, i):
+        return pl.ds(pl.multiple_of(t * step + i * SUB, SUB), SUB)
+
+    def collect(t):
+        into = hot_rows(index_row(receiver, t, step), 0, count)
+        aggregate[...] += dot(into, messages[...])
+
     def forward(t, carry):
-        rows = step_rows(t, step)
         piece(t, step, part_hbm, part, part_sem).wait()
-        hot = hot_columns(slanes[rows, :], count, halo)
-        hidden = part[rows, :].astype(F32) + dot(hot, table[...])
-        active, slope = silu_parts(hidden)
-        slopes[rows, :] = slope.astype(BF)
-        normal, spread = normalise(dot(active.astype(BF), w2[...]))
-        normals[rows, :] = normal.astype(BF)
-        spreads[rows, :] = spread
-        message = jnp.where(live_rows(counts_ref, t, step), normal * gain, 0.0)
         piece(t, step, edges_hbm, edges, edges_sem).wait()
-        eout[rows, :] = (edges[rows, :].astype(F32) + message).astype(BF)
-        into = hot_rows(index_row(receiver, t, step), 0, count)
-        aggregate[...] += dot(into, message.astype(BF))
+        collect(jnp.maximum(t - 1, 0))
+        hidden, centre = {}, {}
+        for i in range(subs + 2):
+            if i < subs:
+                rows = part_of(t, i)
+                hot = hot_columns(slanes[rows, :], count, halo)
+                hidden[i] = part[rows, :].astype(F32) + dot(hot, table[...])
+            if 0 <= i - 1 < subs:
+                active, slope = silu_parts(hidden.pop(i - 1))
+                slopes[part_of(t, i - 1), :] = slope.astype(BF)
+                centre[i - 1] = dot(active.astype(BF), w2c[...])
+            if i >= 2:
+                rows = part_of(t, i - 2)
+                c = centre.pop(i - 2)
+                spread = lax.rsqrt(row_mean(c * c) + 1e-05)
+                normal = c * spread
+                normals[rows, :] = normal.astype(BF)
+                spreads[rows, :] = spread
+                message = jnp.where(live_part(counts_ref, t, step, i - 2), normal * gain, 0.0)
+                eout[rows, :] = (edges[rows, :].astype(F32) + message).astype(BF)
+                messages[(i - 2) * SUB : (i - 1) * SUB, :] = message.astype(BF)
         piece(t, step, eout, edge_out_hbm, eout_sem).start()
         return carry
 
     lax.fori_loop(0, steps, forward, 0)
+    collect(steps - 1)
     for c in later:
         c.wait()
 
@@ -245,24 +294,36 @@
     ends = fetch(last_sem, (node_out, node_out_hbm), (direct, direct_hbm))
     w2t[...] = jnp.transpose(w2[...], (1, 0))
 
+    hgrad[step_rows(0, step), :] = jnp.zeros((step, width), BF)
+
+    def gather_back(t):
+        hg = hgrad[step_rows(t, step), :]
+        sums[...] += dot(hot_rows(index_row(sender, t, step), count, halo), hg)
+
     def backward(t, carry):
-        rows = step_rows(t, step)
-        upper = dot(hot_columns(rlanes[rows, :], 0, count), agrad[...])
         piece(t, step, cot_hbm, cot, cot_sem).wait()
-        live = live_rows(counts_ref, t, step)
-        scaled = jnp.where(live, (upper + cot[rows, :].astype(F32)) * gain, 0.0)
-        grad = norm_back(scaled, normals[rows, :].astype(F32), spreads[rows, :]).astype(BF)
-        hg = (dot(grad, w2t[...]) * slopes[rows, :].astype(F32)).astype(BF)
-        hgrad[rows, :] = hg
-        sums[...] += dot(hot_rows(index_row(sender, t, step), count, halo), hg)
+        gather_back(jnp.maximum(t - 1, 0))
+        upper, grad = {}, {}
+        for i in range(subs + 2):
+            if i < subs:
+                upper[i] = dot(hot_columns(rlanes[part_of(t, i), :], 0, count), agrad[...])
+            if 0 <= i - 1 < subs:
+                rows = part_of(t, i - 1)
+                live = live_part(counts_ref, t, step, i - 1)
+                scaled = jnp.where(live, (upper.pop(i - 1) + cot[rows, :].astype(F32)) * gain, 0.0)
+                grad[i - 1] = norm_back(scaled, normals[rows, :].astype(F32), spreads[rows, :]).astype(BF)
+            if i >= 2:
+                rows = part_of(t, i - 2)
+                hgrad[rows, :] = (dot(grad.pop(i - 2), w2t[...]) * slopes[rows, :].astype(F32)).astype(BF)
         piece(t, step, hgrad, hgrad_hbm, hgrad_sem).start()
         return carry
 
     lax.fori_loop(0, steps, backward, 0)
-    back = dot_nt(sums[...].astype(BF), w1s[...]).astype(BF)
-    for i, ref in enumerate((r0, r1, r2, r3, r4, r5)):
-        ref[...] = back[i * NEAR : (i + 1) * NEAR]
-    rfar[...] = back[NEAR_TOTAL:fed]
+    gather_back(steps - 1)
+    back = dot_nt(sums[...].astype(BF), w1s[...])
+    for i, ref in zip(RETURN_ORDER, (r0, r1, r2, r3, r4, r5)):
+        ref[...] = back[i * NEAR : (i + 1) * NEAR].astype(BF)
+    pack_far(back[NEAR_TOTAL:fed], far_wide, rfar)
     for t in range(steps):
         piece(t, step, eout, edge_out_hbm, eout_sem).wait()
         piece(t, step, hgrad, hgrad_hbm, hgrad_sem).wait()
@@ -272,15 +333,17 @@
 
 def rest_kernel(
     sender_hbm, receiver_hbm, w1_hbm, direct_hbm, hgrad_hbm, cot_hbm, grad_hbm, owned_hbm,
-    sender, receiver, w1, direct, hgrad, cot, sums, w1t, sems, h_sem, c_sem, out_sem, last_sem,
+    sender, receiver, w1, direct, hgrad, cot, sums, w1t, sems, late_sem, h_sem, c_sem, out_sem, last_sem,
 ):
     step = STEP_REST
     steps = hgrad.shape[0] // step
     count, width = direct.shape
-    first = fetch(sems, (sender_hbm, sender), (receiver_hbm, receiver), (w1_hbm, w1), (direct_hbm, direct))
+    top, bottom = pl.ds(0, width), pl.ds(width, 2 * width)
+    first = fetch(sems, (sender_hbm, sender), (receiver_hbm, receiver), (w1_hbm.at[top], w1.at[top]))
     for t in range(steps):
         piece(t, step, hgrad_hbm, hgrad, h_sem).start()
         piece(t, step, cot_hbm, cot, c_sem).start()
+    later = fetch(late_sem, (w1_hbm.at[bottom], w1.at[bottom]), (direct_hbm, direct))
     sums[...] = jnp.zeros_like(sums)
     for c in first:
         c.wait()
@@ -301,6 +364,8 @@
         return carry
 
     lax.fori_loop(0, steps, body, 0)
+    for c in later:
+        c.wait()
     direct[...] = (
         direct[...]
         + dot_nt(sums[:count, :].astype(BF), w1[width : 2 * width, :])
@@ -314,16 +379,15 @@
 
 def final_kernel(
     list_hbm, owned_hbm, n0, n1, n2, n3, n4, n5, far_hbm, out_hbm,
-    slots, owned, returned, out, sems, last_sem,
+    slots, owned, returned, out, far_packed, far_wide, sems, last_sem,
 ):
-    fed = returned.shape[0]
     near = [(n, returned.at[pl.ds(i * NEAR, NEAR)]) for i, n in enumerate((n0, n1, n2, n3, n4, n5))]
-    for c in fetch(
-        sems, (list_hbm, slots), (owned_hbm, owned), *near,
-        (far_hbm, returned.at[pl.ds(NEAR_TOTAL, fed - NEAR_TOTAL)]),
-    ):
-        c.wait()
+    first = fetch(sems, (list_hbm, slots), *near, (far_hbm, far_packed), (owned_hbm, owned))
+    first[0].wait()
     hot = hot_rows(slots[...], 0, owned.shape[0])
+    for c in first[1:]:
+        c.wait()
+    unpack_far(far_packed, far_wide, returned)
     out[...] = (owned[...] + dot(hot, returned[...])).astype(BF)
     for c in fetch(last_sem, (out, out_hbm)):
         c.wait()
@@ -349,14 +413,16 @@
     slots = edges.shape[0]
     halo = send_list.shape[1]
     far_rows = halo - NEAR_TOTAL
+    far_shape = (lax.axis_size(AXES), far_rows * width // 128 // lax.axis_size(AXES), 128)
     padded = -(-halo // 256) * 256
     v = pl.BlockSpec(memory_space=pltpu.VMEM)
-    s = pl.BlockSpec(memory_space=pltpu.SMEM)
     a = pl.BlockSpec(memory_space=pl.ANY)
     sds = jax.ShapeDtypeStruct
     sem = lambda n: pltpu.SemaphoreType.DMA((n,))
-    near_shapes = [sds((NEAR, width), BF)] * 6 + [sds((far_rows, width), BF)]
+    near_shapes = [sds((NEAR, width), BF)] * 6 + [sds(far_shape, BF)]
     big = sds((slots, width), BF)
+    far_packed = VMEM(far_shape, BF)
+    far_wide = VMEM((far_rows * width // 128, 128), F32)
     wide = VMEM((slots, width), BF)
     lanes = VMEM((slots, 128), I16)
     index = VMEM((slots // 128, 128), jnp.int32)
@@ -374,7 +440,7 @@
     ngain = node_gain.reshape(1, width)
 
     leaving = kernel_call(
-        gather_kernel, near_shapes, [a, a], [v] * 7, [block, listed, sem(2)],
+        gather_kernel, near_shapes, [a, a], [v] * 7, [block, listed, far_wide, sem(2)],
         2 * halo * count * width, 2 * MIB,
     )(nodes, send_list)
     arrived = [shifted(leaving[i], near_offset(i)) for i in range(6)]
@@ -384,20 +450,21 @@
     part = kernel_call(
         local_kernel, big, [a] * 5, a,
         [block, index, index, w1, wide, wide, lanes, lanes, VMEM((2 * count, width), BF), sem(4), sem(n), sem(n)],
-        20 * square, 8 * MIB,
+        square, MIB,
     )(nodes, sender, receiver, edge_w1, edges)
 
     n = slots // STEP_MAIN
     outs = kernel_call(
         main_kernel,
         [big, sds((count, width), BF), big] + near_shapes + [sds((count, width), F32)],
-        [s] + [a] * 20,
+        [a] * 21,
         [a, a, a] + [v] * 7 + [a],
-        [VMEM((halo, width), BF), index, index, mat, mat, vec, VMEM((2 * width, width), BF), mat, vec, block, block]
+        [pltpu.SMEM(tile_counts.shape, jnp.int32), far_packed, far_wide,
+         VMEM((halo, width), BF), index, index, mat, mat, vec, VMEM((2 * width, width), BF), mat, vec, block, block]
         + [wide] * 7
         + [lanes, lanes, VMEM((slots, 1), F32), VMEM((padded, width), BF), VMEM((padded, width), F32),
-           block32, block, block, block32, mat]
-        + [sem(12), sem(5)] + [sem(n)] * 5 + [sem(2)],
+           block32, block, block, block32, mat, mat, VMEM((STEP_MAIN, width), BF)]
+        + [sem(13), sem(5)] + [sem(n)] * 5 + [sem(2)],
         50 * square, 20 * MIB,
     )(
         tile_counts, *arrived, far, sender, receiver, edge_w1, edge_w2, gain, node_w1, node_w2, ngain,
@@ -406,19 +473,20 @@
     edge_out, node_out, hgrad = outs[:3]
     back = outs[3:10]
     direct = outs[10]
-    returned = [shifted(back[i], -near_offset(i)) for i in range(6)]
+    made = {i: shifted(back[k], -near_offset(i)) for k, i in enumerate(RETURN_ORDER)}
+    returned = [made[i] for i in range(6)]
     far_back = exchange_far(back[6])
 
     n = slots // STEP_REST
     grad_edges, owned = kernel_call(
         rest_kernel, [big, sds((count, width), F32)], [a] * 6, [a, a],
-        [index, index, w1, block32, wide, wide, VMEM((2 * count, width), F32), mat, sem(4), sem(n), sem(n), sem(n), sem(1)],
-        20 * square, 12 * MIB,
+        [index, index, w1, block32, wide, wide, VMEM((2 * count, width), F32), mat, sem(3), sem(2), sem(n), sem(n), sem(n), sem(1)],
+        square, MIB,
     )(sender, receiver, edge_w1, direct, hgrad, edge_cotangent)
 
     grad_nodes = kernel_call(
         final_kernel, sds((count, width), BF), [a] * 9, a,
-        [listed, block32, VMEM((halo, width), BF), block, sem(9), sem(1)], 2 * square, 3 * MIB,
+        [listed, block32, VMEM((halo, width), BF), block, far_packed, far_wide, sem(9), sem(1)], 2 * square, 3 * MIB,
     )(send_list, owned, *returned, far_back)
     return edge_out, node_out, grad_edges, grad_nodes
 

time: 103 us -> 95 us (0.922)
  local copies, waits for them, and re-layouts: 6.49 us -> 1.49 us
  Pallas kernels: 54.2 us -> 50.9 us
    all_to_all x4 -> x0, local copies, waits for them, and re-layouts: 5.11 us -> none  [exchange_far(): return lax.all_to_all(rows, AXES, split_axis=0, concat_axis=0, tiled=True)]
    pallas_call x1, Pallas kernels: 29.5 us -> 26.9 us  [on_device(): kernel_call(main_kernel, [big, sds((count, width), BF), big] + near_shape...]
    all_to_all x2, starting transfers between devices: 13.8 us -> 15.3 us  [exchange_far(): return lax.all_to_all(rows, AXES, split_axis=0, concat_axis=0, tiled=True)]
    ppermute x12, starting transfers between devices: 26.8 us -> 25.7 us  [shifted(): lax.ppermute(value, AXES, [(s, (s + steps) % count) for s in range(count)])]
  transfers between devices with their start and end apart: 14 -> 14, of which waited for: 0 -> 1; matrix products, arithmetic and copies ran while one was open for 0% -> 0% of each run, Pallas kernels for 19% -> 20%
where the time goes in v2:
time: 95 us; the launch traced here: 94.5 us
  Pallas kernels  50.9 us (54%)
  starting transfers between devices  41 us (43%)
  local copies, waits for them, and re-layouts  1.49 us (2%)
  between operations  1.05 us (1%)
    pallas_call x1, Pallas kernels, on_device(): kernel_call(main_kernel, [big, sds((count, width), BF), big] + near_shape...  26.9 us
    ppermute x12, starting transfers between devices, shifted(): lax.ppermute(value, AXES, [(s, (s + steps) % count) for s in range(count)])  25.7 us
    all_to_all x2, starting transfers between devices, exchange_far(): return lax.all_to_all(rows, AXES, split_axis=0, concat_axis=0, tiled=True)  15.3 us
    pallas_call x1, Pallas kernels, on_device(): kernel_call(local_kernel, big, [a] * 5, a, [block, index, index, w1, wide...  9.35 us
    pallas_call x1, Pallas kernels, on_device(): kernel_call(rest_kernel, [big, sds((count, width), F32)], [a] * 6, [a, a]...  9.18 us
    pallas_call x1, Pallas kernels, on_device(): kernel_call(final_kernel, sds((count, width), BF), [a] * 9, a, [listed, b...  3.05 us
    pallas_call x1, Pallas kernels, on_device(): kernel_call(gather_kernel, near_shapes, [a, a], [v] * 7, [block, listed,...  2.4 us
  transfers between devices with their start and end apart: 14, of which 1 were waited for; matrix products, arithmetic and copies ran while one was open for 0% of the time, Pallas kernels for 20%

profile of v2, /device:TPU:1, one launch (start us, length us, event | category | flops | bytes accessed | tf_op | source)
XLA Modules:
  0.0 94.5 jit_solution(3196032992025424345)
XLA Ops:
  0.6 2.4 %shard_map.165 = (bf16[80,512]{1,0:T(8,128)(2,1)}, bf16[80,512]{1,0:T(8,128)(2,1)}, bf16[80,512]{1,0:T(8,128)(2,1)}, bf16[80,512]{1,0:T(8,128)(2,1)}, bf16[80,51...) custom-call(bf16[512,512]{1,0:T(8,128)(2,1)} %nodes_hbm.5, s32[1,736]{1,0:T(1,128)} %list_hbm.3), custom_call_target="tpu_custom_call" | custom-call | flops 385875968 | bytes 2097152 | tf_op jit(solution)/shard_map/pallas_call | solution.py:442
  3.0 11.5 %all-to-all-start = ((bf16[128,8,128]{2,1,0:T(8,128)(2,1)}), bf16[128,8,128]{2,1,0:T(8,128)(2,1)S(1)}, u32[]{:S(2)}, u32[]{:S(2)}) async-start(bf16[128,8,128]{2,1,0:T(8,128)(2,1)} %get-tuple-element.30), calls=%async_computation | async-start | bytes 524288 | tf_op jit(solution)/shard_map/all_to_all | solution.py:37
  14.6 1.7 %collective-permute-start = (bf16[80,512]{1,0:T(8,128)(2,1)}, bf16[80,512]{1,0:T(8,128)(2,1)S(1)}, u32[]{:S(2)}, u32[]{:S(2)}) collective-permute-start(bf16[80,512]{1,0:T(8,128)(2,1)} %get-tuple-element.24), channel_id=1, source_target_pairs={{0,1},{1,2},{2,3},{3,4},{4,5},{5,6},{6,7},{7,8},{8,9},{9,10},{10,1... | collective-permute-start | bytes 245768 | tf_op jit(solution)/shard_map/ppermute | solution.py:33
  16.3 1.2 %collective-permute-start.1 = (bf16[80,512]{1,0:T(8,128)(2,1)}, bf16[80,512]{1,0:T(8,128)(2,1)S(1)}, u32[]{:S(2)}, u32[]{:S(2)}) collective-permute-start(bf16[80,512]{1,0:T(8,128)(2,1)} %get-tuple-element.25), channel_id=1, source_target_pairs={{0,2},{1,3},{2,4},{3,5},{4,6},{5,7},{6,8},{7,9},{8,10},{9,11},{10,... | collective-permute-start | bytes 245768 | tf_op jit(solution)/shard_map/ppermute | solution.py:33
  17.4 1.7 %collective-permute-start.2 = (bf16[80,512]{1,0:T(8,128)(2,1)}, bf16[80,512]{1,0:T(8,128)(2,1)S(1)}, u32[]{:S(2)}, u32[]{:S(2)}) collective-permute-start(bf16[80,512]{1,0:T(8,128)(2,1)} %get-tuple-element.26), channel_id=1, source_target_pairs={{0,3},{1,4},{2,5},{3,6},{4,7},{5,8},{6,9},{7,10},{8,11},{9,12},{10... | collective-permute-start | bytes 245768 | tf_op jit(solution)/shard_map/ppermute | solution.py:33
  19.1 0.0 collective-permute-start.3
  19.1 5.6 %collective-permute-start.4 = (bf16[80,512]{1,0:T(8,128)(2,1)}, bf16[80,512]{1,0:T(8,128)(2,1)S(1)}, u32[]{:S(2)}, u32[]{:S(2)}) collective-permute-start(bf16[80,512]{1,0:T(8,128)(2,1)} %get-tuple-element.28), channel_id=1, source_target_pairs={{0,126},{1,127},{2,0},{3,1},{4,2},{5,3},{6,4},{7,5},{8,6},{9,7},{1... | collective-permute-start | bytes 245768 | tf_op jit(solution)/shard_map/ppermute | solution.py:33
  24.7 0.0 collective-permute-done.n0
  24.7 0.0 copy-start.8
  24.7 4.3 %collective-permute-start.5 = (bf16[80,512]{1,0:T(8,128)(2,1)}, bf16[80,512]{1,0:T(8,128)(2,1)S(1)}, u32[]{:S(2)}, u32[]{:S(2)}) collective-permute-start(bf16[80,512]{1,0:T(8,128)(2,1)} %get-tuple-element.29), channel_id=1, source_target_pairs={{0,125},{1,126},{2,127},{3,0},{4,1},{5,2},{6,3},{7,4},{8,5},{9,6},... | collective-permute-start | bytes 245768 | tf_op jit(solution)/shard_map/ppermute | solution.py:33
  29.0 9.3 %shard_map.166.part_hbm = bf16[3072,512]{1,0:T(8,128)(2,1)} custom-call(bf16[512,512]{1,0:T(8,128)(2,1)} %nodes_hbm.5, s32[24,128]{1,0:T(8,128)} %bitcast.4, s32[24,128]{1,0:T(8,128)} %bitcast.7, bf16[1536,512]{1,0:T(8,128)(2,1)} %w1_hbm.5, bf16[3072,512]{1,0:T(8,128)(2,1)} %edges_hbm.3), custom_call_target="tpu_custom_call" | custom-call | flops 268435456 | bytes 1048576 | tf_op jit(solution)/shard_map/pallas_call | solution.py:450
  38.4 0.0 copy-done.8
  38.4 0.0 collective-permute-done.1.n1
  38.4 0.0 copy-start.9
  38.4 0.0 collective-permute-done.2.n2
  38.4 0.0 copy-start.10
  38.4 0.0 collective-permute-done.3.n3
  38.4 0.0 copy-start.11
  38.4 0.0 collective-permute-done.4.n4
  38.5 0.0 copy-start.12
  38.5 0.0 collective-permute-done.5.n5
  38.5 0.0 copy-start.13
  38.5 0.0 all-to-all-done.far_hbm
  38.5 0.0 copy-start.1
  38.5 0.5 copy-done.9
  39.0 0.0 copy-done.10
  39.1 0.1 copy-done.11
  39.1 0.0 copy-done.12
  39.1 0.1 copy-done.13
  39.2 0.0 copy-done.1
  39.2 26.9 %shard_map.167 = (bf16[3072,512]{1,0:T(8,128)(2,1)}, bf16[512,512]{1,0:T(8,128)(2,1)}, bf16[3072,512]{1,0:T(8,128)(2,1)}, bf16[80,512]{1,0:T(8,128)(2,1)}, bf16[...) custom-call(s32[12]{0:T(128)} %counts_hbm.1, ...), custom_call_target="tpu_custom_call" | custom-call | flops 13421772800 | bytes 20971520 | tf_op jit(solution)/shard_map/pallas_call | solution.py:457
  66.2 3.8 %all-to-all-start.1 = ((bf16[128,8,128]{2,1,0:T(8,128)(2,1)}), bf16[128,8,128]{2,1,0:T(8,128)(2,1)S(1)}, u32[]{:S(2)}, u32[]{:S(2)}) async-start(bf16[128,8,128]{2,1,0:T(8,128)(2,1)} %get-tuple-element.43), calls=%async_computation.1 | async-start | bytes 524288 | tf_op jit(solution)/shard_map/all_to_all | solution.py:37
  70.0 0.3 collective-permute-start.6
  70.3 7.0 %collective-permute-start.7 = (bf16[80,512]{1,0:T(8,128)(2,1)}, bf16[80,512]{1,0:T(8,128)(2,1)S(1)}, u32[]{:S(2)}, u32[]{:S(2)}) collective-permute-start(bf16[80,512]{1,0:T(8,128)(2,1)} %get-tuple-element.38), channel_id=1, source_target_pairs={{0,126},{1,127},{2,0},{3,1},{4,2},{5,3},{6,4},{7,5},{8,6},{9,7},{1... | collective-permute-start | bytes 245768 | tf_op jit(solution)/shard_map/ppermute | solution.py:33
  77.3 0.9 collective-permute-start.8
  78.2 0.7 collective-permute-start.9
  78.9 1.3 %collective-permute-start.10 = (bf16[80,512]{1,0:T(8,128)(2,1)}, bf16[80,512]{1,0:T(8,128)(2,1)S(1)}, u32[]{:S(2)}, u32[]{:S(2)}) collective-permute-start(bf16[80,512]{1,0:T(8,128)(2,1)} %get-tuple-element.41), channel_id=1, source_target_pairs={{0,2},{1,3},{2,4},{3,5},{4,6},{5,7},{6,8},{7,9},{8,10},{9,11},{10,... | collective-permute-start | bytes 245768 | tf_op jit(solution)/shard_map/ppermute | solution.py:33
  80.2 0.0 collective-permute-done.6.n0
  80.2 0.0 copy-start.2
  80.2 1.0 %collective-permute-start.11 = (bf16[80,512]{1,0:T(8,128)(2,1)}, bf16[80,512]{1,0:T(8,128)(2,1)S(1)}, u32[]{:S(2)}, u32[]{:S(2)}) collective-permute-start(bf16[80,512]{1,0:T(8,128)(2,1)} %get-tuple-element.42), channel_id=1, source_target_pairs={{0,3},{1,4},{2,5},{3,6},{4,7},{5,8},{6,9},{7,10},{8,11},{9,12},{10... | collective-permute-start | bytes 245768 | tf_op jit(solution)/shard_map/ppermute | solution.py:33
  81.2 9.2 %shard_map.168 = (bf16[3072,512]{1,0:T(8,128)(2,1)}, f32[512,512]{1,0:T(8,128)}) custom-call(s32[24,128]{1,0:T(8,128)} %bitcast.6, s32[24,128]{1,0:T(8,128)} %bitcast.9, bf16[1536,512]{1,0:T(8,128)(2,1)} %w1_hbm.5, f32[512,512]{1,0:T(8,128)} %get-tuple-element.33.direct_hbm, bf16[3072,512]{1,0:T(8,128)(2,1)} %get-tuple-element.34.hgrad_hbm, ...), custom_call_target="tpu_custom_call" | custom-call | flops 268435456 | bytes 1048576 | tf_op jit(solution)/shard_map/pallas_call | solution.py:481
  90.4 0.0 copy-done.2
  90.4 0.0 collective-permute-done.7.n1
  90.4 0.0 copy-start.3
  90.4 0.0 collective-permute-done.8.n2
  90.4 0.0 copy-start.4
  90.4 0.0 collective-permute-done.9.n3
  90.5 0.0 copy-start.5
  90.5 0.0 collective-permute-done.10.n4
  90.5 0.0 copy-start.6
  90.5 0.1 collective-permute-done.11.n5
  90.6 0.0 copy-start.7
  90.6 0.0 all-to-all-done.1.far_hbm
  90.6 0.0 copy-start
  90.6 0.5 copy-done.3
  91.0 0.0 copy-done.4
  91.1 0.0 copy-done.5
  91.1 0.0 copy-done.6
  91.1 0.1 copy-done.7
  91.2 0.1 copy-done
  91.3 3.1 %shard_map.169 = bf16[512,512]{1,0:T(8,128)(2,1)} custom-call(s32[1,736]{1,0:T(1,128)} %list_hbm.3, f32[512,512]{1,0:T(8,128)} %get-tuple-element.36.owned_hbm, bf16[80,512]{1,0:T(8,128)(2,1)} %copy-done.2, bf16[80,512]{1,0:T(8,128)(2,1)} %copy-done.3, bf16[80,512]{1,0:T(8,128)(2,1)} %copy-done.4, bf16[80,512]{1,0:T(8,128)(2,1)} %copy-done.5, ...), custom_call_target="tpu_custom_call" | custom-call | flops 536870912 | bytes 3145728 | tf_op jit(solution)/shard_map/pallas_call | solution.py:487
Async XLA Ops:
  3.0 35.4 %all-to-all-start = ((bf16[128,8,128]{2,1,0:T(8,128)(2,1)}), bf16[128,8,128]{2,1,0:T(8,128)(2,1)S(1)}, u32[]{:S(2)}, u32[]{:S(2)}) async-start(bf16[128,8,128]{2,1,0:T(8,128)(2,1)} %get-tuple-element.30), calls=%async_computation | async-start | bytes 524288 | tf_op jit(solution)/shard_map/all_to_all | solution.py:37
  14.6 10.2 %collective-permute-start = (bf16[80,512]{1,0:T(8,128)(2,1)}, bf16[80,512]{1,0:T(8,128)(2,1)S(1)}, u32[]{:S(2)}, u32[]{:S(2)}) collective-permute-start(bf16[80,512]{1,0:T(8,128)(2,1)} %get-tuple-element.24), channel_id=1, source_target_pairs={{0,1},{1,2},{2,3},{3,4},{4,5},{5,6},{6,7},{7,8},{8,9},{9,10},{10,1... | collective-permute-start | bytes 245768 | tf_op jit(solution)/shard_map/ppermute | solution.py:33
  16.3 22.1 %collective-permute-start.1 = (bf16[80,512]{1,0:T(8,128)(2,1)}, bf16[80,512]{1,0:T(8,128)(2,1)S(1)}, u32[]{:S(2)}, u32[]{:S(2)}) collective-permute-start(bf16[80,512]{1,0:T(8,128)(2,1)} %get-tuple-element.25), channel_id=1, source_target_pairs={{0,2},{1,3},{2,4},{3,5},{4,6},{5,7},{6,8},{7,9},{8,10},{9,11},{10,... | collective-permute-start | bytes 245768 | tf_op jit(solution)/shard_map/ppermute | solution.py:33
  17.4 21.0 %collective-permute-start.2 = (bf16[80,512]{1,0:T(8,128)(2,1)}, bf16[80,512]{1,0:T(8,128)(2,1)S(1)}, u32[]{:S(2)}, u32[]{:S(2)}) collective-permute-start(bf16[80,512]{1,0:T(8,128)(2,1)} %get-tuple-element.26), channel_id=1, source_target_pairs={{0,3},{1,4},{2,5},{3,6},{4,7},{5,8},{6,9},{7,10},{8,11},{9,12},{10... | collective-permute-start | bytes 245768 | tf_op jit(solution)/shard_map/ppermute | solution.py:33
  19.1 19.3 %collective-permute-start.3 = (bf16[80,512]{1,0:T(8,128)(2,1)}, bf16[80,512]{1,0:T(8,128)(2,1)S(1)}, u32[]{:S(2)}, u32[]{:S(2)}) collective-permute-start(bf16[80,512]{1,0:T(8,128)(2,1)} %get-tuple-element.27), channel_id=1, source_target_pairs={{0,127},{1,0},{2,1},{3,2},{4,3},{5,4},{6,5},{7,6},{8,7},{9,8},{10,... | collective-permute-start | bytes 245768 | tf_op jit(solution)/shard_map/ppermute | solution.py:33
  19.1 19.3 %collective-permute-start.4 = (bf16[80,512]{1,0:T(8,128)(2,1)}, bf16[80,512]{1,0:T(8,128)(2,1)S(1)}, u32[]{:S(2)}, u32[]{:S(2)}) collective-permute-start(bf16[80,512]{1,0:T(8,128)(2,1)} %get-tuple-element.28), channel_id=1, source_target_pairs={{0,126},{1,127},{2,0},{3,1},{4,2},{5,3},{6,4},{7,5},{8,6},{9,7},{1... | collective-permute-start | bytes 245768 | tf_op jit(solution)/shard_map/ppermute | solution.py:33
  24.7 13.6 %copy-start.8 = (bf16[80,512]{1,0:T(8,128)(2,1)}, bf16[80,512]{1,0:T(8,128)(2,1)S(1)}, u32[]{:S(2)}) copy-start(bf16[80,512]{1,0:T(8,128)(2,1)S(1)} %collective-permute-done.n0) | copy-start | bytes 245764
  24.7 13.7 %collective-permute-start.5 = (bf16[80,512]{1,0:T(8,128)(2,1)}, bf16[80,512]{1,0:T(8,128)(2,1)S(1)}, u32[]{:S(2)}, u32[]{:S(2)}) collective-permute-start(bf16[80,512]{1,0:T(8,128)(2,1)} %get-tuple-element.29), channel_id=1, source_target_pairs={{0,125},{1,126},{2,127},{3,0},{4,1},{5,2},{6,3},{7,4},{8,5},{9,6},... | collective-permute-start | bytes 245768 | tf_op jit(solution)/shard_map/ppermute | solution.py:33
  38.4 0.6 copy-start.9
  38.4 0.6 copy-start.10
  38.4 0.7 copy-start.11
  38.5 0.7 copy-start.12
  38.5 0.7 copy-start.13
  38.5 0.7 copy-start.1
  66.2 24.4 %all-to-all-start.1 = ((bf16[128,8,128]{2,1,0:T(8,128)(2,1)}), bf16[128,8,128]{2,1,0:T(8,128)(2,1)S(1)}, u32[]{:S(2)}, u32[]{:S(2)}) async-start(bf16[128,8,128]{2,1,0:T(8,128)(2,1)} %get-tuple-element.43), calls=%async_computation.1 | async-start | bytes 524288 | tf_op jit(solution)/shard_map/all_to_all | solution.py:37
  70.0 10.3 %collective-permute-start.6 = (bf16[80,512]{1,0:T(8,128)(2,1)}, bf16[80,512]{1,0:T(8,128)(2,1)S(1)}, u32[]{:S(2)}, u32[]{:S(2)}) collective-permute-start(bf16[80,512]{1,0:T(8,128)(2,1)} %get-tuple-element.37), channel_id=1, source_target_pairs={{0,127},{1,0},{2,1},{3,2},{4,3},{5,4},{6,5},{7,6},{8,7},{9,8},{10,... | collective-permute-start | bytes 245768 | tf_op jit(solution)/shard_map/ppermute | solution.py:33
  70.3 20.2 %collective-permute-start.7 = (bf16[80,512]{1,0:T(8,128)(2,1)}, bf16[80,512]{1,0:T(8,128)(2,1)S(1)}, u32[]{:S(2)}, u32[]{:S(2)}) collective-permute-start(bf16[80,512]{1,0:T(8,128)(2,1)} %get-tuple-element.38), channel_id=1, source_target_pairs={{0,126},{1,127},{2,0},{3,1},{4,2},{5,3},{6,4},{7,5},{8,6},{9,7},{1... | collective-permute-start | bytes 245768 | tf_op jit(solution)/shard_map/ppermute | solution.py:33
  77.3 13.1 %collective-permute-start.8 = (bf16[80,512]{1,0:T(8,128)(2,1)}, bf16[80,512]{1,0:T(8,128)(2,1)S(1)}, u32[]{:S(2)}, u32[]{:S(2)}) collective-permute-start(bf16[80,512]{1,0:T(8,128)(2,1)} %get-tuple-element.39), channel_id=1, source_target_pairs={{0,125},{1,126},{2,127},{3,0},{4,1},{5,2},{6,3},{7,4},{8,5},{9,6},... | collective-permute-start | bytes 245768 | tf_op jit(solution)/shard_map/ppermute | solution.py:33
  78.2 12.2 %collective-permute-start.9 = (bf16[80,512]{1,0:T(8,128)(2,1)}, bf16[80,512]{1,0:T(8,128)(2,1)S(1)}, u32[]{:S(2)}, u32[]{:S(2)}) collective-permute-start(bf16[80,512]{1,0:T(8,128)(2,1)} %get-tuple-element.40), channel_id=1, source_target_pairs={{0,1},{1,2},{2,3},{3,4},{4,5},{5,6},{6,7},{7,8},{8,9},{9,10},{10,1... | collective-permute-start | bytes 245768 | tf_op jit(solution)/shard_map/ppermute | solution.py:33
  78.9 11.5 %collective-permute-start.10 = (bf16[80,512]{1,0:T(8,128)(2,1)}, bf16[80,512]{1,0:T(8,128)(2,1)S(1)}, u32[]{:S(2)}, u32[]{:S(2)}) collective-permute-start(bf16[80,512]{1,0:T(8,128)(2,1)} %get-tuple-element.41), channel_id=1, source_target_pairs={{0,2},{1,3},{2,4},{3,5},{4,6},{5,7},{6,8},{7,9},{8,10},{9,11},{10,... | collective-permute-start | bytes 245768 | tf_op jit(solution)/shard_map/ppermute | solution.py:33
  80.2 10.2 %copy-start.2 = (bf16[80,512]{1,0:T(8,128)(2,1)}, bf16[80,512]{1,0:T(8,128)(2,1)S(1)}, u32[]{:S(2)}) copy-start(bf16[80,512]{1,0:T(8,128)(2,1)S(1)} %collective-permute-done.6.n0) | copy-start | bytes 245764
  80.2 10.4 %collective-permute-start.11 = (bf16[80,512]{1,0:T(8,128)(2,1)}, bf16[80,512]{1,0:T(8,128)(2,1)S(1)}, u32[]{:S(2)}, u32[]{:S(2)}) collective-permute-start(bf16[80,512]{1,0:T(8,128)(2,1)} %get-tuple-element.42), channel_id=1, source_target_pairs={{0,3},{1,4},{2,5},{3,6},{4,7},{5,8},{6,9},{7,10},{8,11},{9,12},{10... | collective-permute-start | bytes 245768 | tf_op jit(solution)/shard_map/ppermute | solution.py:33
  90.4 0.6 copy-start.3
  90.4 0.6 copy-start.4
  90.5 0.7 copy-start.5
  90.5 0.7 copy-start.6
  90.6 0.6 copy-start.7
  90.6 0.7 copy-start

commit v3 on v2

--- a/solution.py
+++ b/solution.py
@@ -21,7 +21,8 @@
 SUB = 256
 STEP_LOCAL = 1024
 STEP_MAIN = 1024
-STEP_REST = 1536
+STEP_REST = 1024
+WINDOW = 256
 
 
 def near_offset(neighbour):
@@ -97,6 +98,13 @@
     sigma = 0.5 * jnp.tanh(0.5 * x) + 0.5
     active = x * sigma
     return active, sigma + active * (1.0 - sigma)
+
+
+def receiver_window(ids_ref, t, step, count):
+    per = step // 128
+    first, last = ids_ref[t * per, 0], ids_ref[t * per + per - 1, 127]
+    base = jnp.minimum(lax.shift_left(lax.shift_right_logical(first, 4), 4), count - WINDOW)
+    return base, last - base < WINDOW
 
 
 def step_rows(t, step):
@@ -163,12 +171,12 @@
 
 def local_kernel(
     nodes_hbm, sender_hbm, receiver_hbm, w1_hbm, edges_hbm, part_hbm,
-    nodes, sender, receiver, w1, edges, part, slanes, rlanes, table, sems, in_sem, out_sem,
+    nodes, sender, receiver, w1, edges, part, slanes, rlanes, table, window, ids, sems, in_sem, out_sem,
 ):
     step = STEP_LOCAL
     steps = edges.shape[0] // step
     count, width = nodes.shape
-    first = fetch(sems, (sender_hbm, sender), (receiver_hbm, receiver), (nodes_hbm, nodes), (w1_hbm, w1))
+    first = fetch(sems, (sender_hbm, sender), (receiver_hbm, receiver), (nodes_hbm, nodes), (w1_hbm, w1), (receiver_hbm, ids))
     for t in range(steps):
         piece(t, step, edges_hbm, edges, in_sem).start()
     for c in first[:2]:
@@ -183,11 +191,26 @@
     def body(t, carry):
         rows = step_rows(t, step)
         piece(t, step, edges_hbm, edges, in_sem).wait()
-        hot = jnp.concatenate(
-            [hot_columns(slanes[rows, :], 0, count), hot_columns(rlanes[rows, :], 0, count)], axis=1
-        )
-        total = dot(hot, table[...]) + dot(edges[rows, :], w1[:width, :])
-        part[rows, :] = total.astype(BF)
+        base, fits = receiver_window(ids, t, step, count)
+
+        @pl.when(fits)
+        def _():
+            window[:count, :] = table[:count, :]
+            window[count : count + WINDOW, :] = table[pl.ds(pl.multiple_of(count + base, 16), WINDOW), :]
+            window[count + WINDOW :, :] = w1[:width, :]
+            near = rlanes[rows, :] - base.astype(I16)
+            joined = jnp.concatenate(
+                [hot_columns(slanes[rows, :], 0, count), hot_columns(near, 0, WINDOW), edges[rows, :]], axis=1
+            )
+            part[rows, :] = dot(joined, window[...]).astype(BF)
+
+        @pl.when(jnp.logical_not(fits))
+        def _():
+            hot = jnp.concatenate(
+                [hot_columns(slanes[rows, :], 0, count), hot_columns(rlanes[rows, :], 0, count)], axis=1
+            )
+            part[rows, :] = (dot(hot, table[...]) + dot(edges[rows, :], w1[:width, :])).astype(BF)
+
         piece(t, step, part, part_hbm, out_sem).start()
         return carry
 
@@ -333,13 +356,13 @@
 
 def rest_kernel(
     sender_hbm, receiver_hbm, w1_hbm, direct_hbm, hgrad_hbm, cot_hbm, grad_hbm, owned_hbm,
-    sender, receiver, w1, direct, hgrad, cot, sums, w1t, sems, late_sem, h_sem, c_sem, out_sem, last_sem,
+    sender, receiver, w1, direct, hgrad, cot, sums, w1t, ids, sems, late_sem, h_sem, c_sem, out_sem, last_sem,
 ):
     step = STEP_REST
     steps = hgrad.shape[0] // step
     count, width = direct.shape
     top, bottom = pl.ds(0, width), pl.ds(width, 2 * width)
-    first = fetch(sems, (sender_hbm, sender), (receiver_hbm, receiver), (w1_hbm.at[top], w1.at[top]))
+    first = fetch(sems, (sender_hbm, sender), (receiver_hbm, receiver), (w1_hbm.at[top], w1.at[top]), (receiver_hbm, ids))
     for t in range(steps):
         piece(t, step, hgrad_hbm, hgrad, h_sem).start()
         piece(t, step, cot_hbm, cot, c_sem).start()
@@ -355,11 +378,26 @@
         piece(t, step, cot_hbm, cot, c_sem).wait()
         hg = hgrad[rows, :]
         cot[rows, :] = (cot[rows, :].astype(F32) + dot(hg, w1t[...])).astype(BF)
-        hot = jnp.concatenate(
-            [hot_rows(index_row(sender, t, step), 0, count), hot_rows(index_row(receiver, t, step), 0, count)],
-            axis=0,
-        )
-        sums[...] += dot(hot, hg)
+        base, fits = receiver_window(ids, t, step, count)
+
+        @pl.when(fits)
+        def _():
+            hot = jnp.concatenate(
+                [hot_rows(index_row(sender, t, step), 0, count), hot_rows(index_row(receiver, t, step), base, WINDOW)],
+                axis=0,
+            )
+            total = dot(hot, hg)
+            sums[:count, :] += total[:count]
+            sums[pl.ds(pl.multiple_of(count + base, 16), WINDOW), :] += total[count:]
+
+        @pl.when(jnp.logical_not(fits))
+        def _():
+            hot = jnp.concatenate(
+                [hot_rows(index_row(sender, t, step), 0, count), hot_rows(index_row(receiver, t, step), 0, count)],
+                axis=0,
+            )
+            sums[...] += dot(hot, hg)
+
         piece(t, step, cot, grad_hbm, out_sem).start()
         return carry
 
@@ -449,7 +487,8 @@
     n = slots // STEP_LOCAL
     part = kernel_call(
         local_kernel, big, [a] * 5, a,
-        [block, index, index, w1, wide, wide, lanes, lanes, VMEM((2 * count, width), BF), sem(4), sem(n), sem(n)],
+        [block, index, index, w1, wide, wide, lanes, lanes, VMEM((2 * count, width), BF), VMEM((count + WINDOW + width, width), BF),
+         pltpu.SMEM((slots // 128, 128), jnp.int32), sem(5), sem(n), sem(n)],
         square, MIB,
     )(nodes, sender, receiver, edge_w1, edges)
 
@@ -480,7 +519,7 @@
     n = slots // STEP_REST
     grad_edges, owned = kernel_call(
         rest_kernel, [big, sds((count, width), F32)], [a] * 6, [a, a],
-        [index, index, w1, block32, wide, wide, VMEM((2 * count, width), F32), mat, sem(3), sem(2), sem(n), sem(n), sem(n), sem(1)],
+        [index, index, w1, block32, wide, wide, VMEM((2 * count, width), F32), mat, pltpu.SMEM((slots // 128, 128), jnp.int32), sem(4), sem(2), sem(n), sem(n), sem(n), sem(1)],
         square, MIB,
     )(sender, receiver, edge_w1, direct, hgrad, edge_cotangent)
 

time: 95 us -> 94.1 us (level)
  Pallas kernels: 50.9 us -> 49.5 us
  transfers between devices with their start and end apart: 14 -> 14, of which waited for: 1 -> 1; matrix products, arithmetic and copies ran while one was open for 0% -> 0% of each run, Pallas kernels for 20% -> 18%
where the time goes in v3:
time: 94.1 us; the launch traced here: 93.6 us
  Pallas kernels  49.5 us (53%)
  starting transfers between devices  40.9 us (43%)
  local copies, waits for them, and re-layouts  1.47 us (2%)
  between operations  1.07 us (1%)
    pallas_call x1, Pallas kernels, on_device(): kernel_call(main_kernel, [big, sds((count, width), BF), big] + near_shape...  26.9 us
    ppermute x12, starting transfers between devices, shifted(): lax.ppermute(value, AXES, [(s, (s + steps) % count) for s in range(count)])  25.7 us
    all_to_all x2, starting transfers between devices, exchange_far(): return lax.all_to_all(rows, AXES, split_axis=0, concat_axis=0, tiled=True)  15.3 us
    pallas_call x1, Pallas kernels, on_device(): kernel_call(rest_kernel, [big, sds((count, width), F32)], [a] * 6, [a, a]...  8.66 us
    pallas_call x1, Pallas kernels, on_device(): kernel_call(local_kernel, big, [a] * 5, a, [block, index, index, w1, wide...  8.47 us
    pallas_call x1, Pallas kernels, on_device(): kernel_call(final_kernel, sds((count, width), BF), [a] * 9, a, [listed, b...  3.05 us
    pallas_call x1, Pallas kernels, on_device(): kernel_call(gather_kernel, near_shapes, [a, a], [v] * 7, [block, listed,...  2.4 us
  transfers between devices with their start and end apart: 14, of which 1 were waited for; matrix products, arithmetic and copies ran while one was open for 0% of the time, Pallas kernels for 18%

profile of v3, /device:TPU:1, one launch (start us, length us, event | category | flops | bytes accessed | tf_op | source)
XLA Modules:
  0.0 93.6 jit_solution(3893608022578744695)
XLA Ops:
  0.6 2.4 %shard_map.165 = (bf16[80,512]{1,0:T(8,128)(2,1)}, bf16[80,512]{1,0:T(8,128)(2,1)}, bf16[80,512]{1,0:T(8,128)(2,1)}, bf16[80,512]{1,0:T(8,128)(2,1)}, bf16[80,51...) custom-call(bf16[512,512]{1,0:T(8,128)(2,1)} %nodes_hbm.5, s32[1,736]{1,0:T(1,128)} %list_hbm.3), custom_call_target="tpu_custom_call" | custom-call | flops 385875968 | bytes 2097152 | tf_op jit(solution)/shard_map/pallas_call | solution.py:480
  3.0 11.5 %all-to-all-start = ((bf16[128,8,128]{2,1,0:T(8,128)(2,1)}), bf16[128,8,128]{2,1,0:T(8,128)(2,1)S(1)}, u32[]{:S(2)}, u32[]{:S(2)}) async-start(bf16[128,8,128]{2,1,0:T(8,128)(2,1)} %get-tuple-element.30), calls=%async_computation | async-start | bytes 524288 | tf_op jit(solution)/shard_map/all_to_all | solution.py:38
  14.6 1.7 %collective-permute-start = (bf16[80,512]{1,0:T(8,128)(2,1)}, bf16[80,512]{1,0:T(8,128)(2,1)S(1)}, u32[]{:S(2)}, u32[]{:S(2)}) collective-permute-start(bf16[80,512]{1,0:T(8,128)(2,1)} %get-tuple-element.24), channel_id=1, source_target_pairs={{0,1},{1,2},{2,3},{3,4},{4,5},{5,6},{6,7},{7,8},{8,9},{9,10},{10,1... | collective-permute-start | bytes 245768 | tf_op jit(solution)/shard_map/ppermute | solution.py:34
  16.3 1.2 %collective-permute-start.1 = (bf16[80,512]{1,0:T(8,128)(2,1)}, bf16[80,512]{1,0:T(8,128)(2,1)S(1)}, u32[]{:S(2)}, u32[]{:S(2)}) collective-permute-start(bf16[80,512]{1,0:T(8,128)(2,1)} %get-tuple-element.25), channel_id=1, source_target_pairs={{0,2},{1,3},{2,4},{3,5},{4,6},{5,7},{6,8},{7,9},{8,10},{9,11},{10,... | collective-permute-start | bytes 245768 | tf_op jit(solution)/shard_map/ppermute | solution.py:34
  17.4 1.7 %collective-permute-start.2 = (bf16[80,512]{1,0:T(8,128)(2,1)}, bf16[80,512]{1,0:T(8,128)(2,1)S(1)}, u32[]{:S(2)}, u32[]{:S(2)}) collective-permute-start(bf16[80,512]{1,0:T(8,128)(2,1)} %get-tuple-element.26), channel_id=1, source_target_pairs={{0,3},{1,4},{2,5},{3,6},{4,7},{5,8},{6,9},{7,10},{8,11},{9,12},{10... | collective-permute-start | bytes 245768 | tf_op jit(solution)/shard_map/ppermute | solution.py:34
  19.1 0.0 collective-permute-start.3
  19.1 5.6 %collective-permute-start.4 = (bf16[80,512]{1,0:T(8,128)(2,1)}, bf16[80,512]{1,0:T(8,128)(2,1)S(1)}, u32[]{:S(2)}, u32[]{:S(2)}) collective-permute-start(bf16[80,512]{1,0:T(8,128)(2,1)} %get-tuple-element.28), channel_id=1, source_target_pairs={{0,126},{1,127},{2,0},{3,1},{4,2},{5,3},{6,4},{7,5},{8,6},{9,7},{1... | collective-permute-start | bytes 245768 | tf_op jit(solution)/shard_map/ppermute | solution.py:34
  24.7 0.0 collective-permute-done.n0
  24.7 0.0 copy-start.8
  24.7 4.3 %collective-permute-start.5 = (bf16[80,512]{1,0:T(8,128)(2,1)}, bf16[80,512]{1,0:T(8,128)(2,1)S(1)}, u32[]{:S(2)}, u32[]{:S(2)}) collective-permute-start(bf16[80,512]{1,0:T(8,128)(2,1)} %get-tuple-element.29), channel_id=1, source_target_pairs={{0,125},{1,126},{2,127},{3,0},{4,1},{5,2},{6,3},{7,4},{8,5},{9,6},... | collective-permute-start | bytes 245768 | tf_op jit(solution)/shard_map/ppermute | solution.py:34
  29.0 8.5 %shard_map.166.part_hbm = bf16[3072,512]{1,0:T(8,128)(2,1)} custom-call(bf16[512,512]{1,0:T(8,128)(2,1)} %nodes_hbm.5, s32[24,128]{1,0:T(8,128)} %bitcast.4, s32[24,128]{1,0:T(8,128)} %bitcast.7, bf16[1536,512]{1,0:T(8,128)(2,1)} %w1_hbm.5, bf16[3072,512]{1,0:T(8,128)(2,1)} %edges_hbm.3), custom_call_target="tpu_custom_call" | custom-call | flops 268435456 | bytes 1048576 | tf_op jit(solution)/shard_map/pallas_call | solution.py:488
  37.5 0.0 copy-done.8
  37.5 0.0 collective-permute-done.1.n1
  37.5 0.0 copy-start.9
  37.5 0.0 collective-permute-done.2.n2
  37.5 0.0 copy-start.10
  37.5 0.0 collective-permute-done.3.n3
  37.5 0.0 copy-start.11
  37.6 0.0 collective-permute-done.4.n4
  37.6 0.0 copy-start.12
  37.6 0.0 collective-permute-done.5.n5
  37.6 0.0 copy-start.13
  37.6 0.0 all-to-all-done.far_hbm
  37.6 0.0 copy-start.1
  37.6 0.5 copy-done.9
  38.1 0.0 copy-done.10
  38.2 0.1 copy-done.11
  38.2 0.0 copy-done.12
  38.2 0.1 copy-done.13
  38.3 0.0 copy-done.1
  38.3 26.9 %shard_map.167 = (bf16[3072,512]{1,0:T(8,128)(2,1)}, bf16[512,512]{1,0:T(8,128)(2,1)}, bf16[3072,512]{1,0:T(8,128)(2,1)}, bf16[80,512]{1,0:T(8,128)(2,1)}, bf16[...) custom-call(s32[12]{0:T(128)} %counts_hbm.1, ...), custom_call_target="tpu_custom_call" | custom-call | flops 13421772800 | bytes 20971520 | tf_op jit(solution)/shard_map/pallas_call | solution.py:496
  65.3 3.8 %all-to-all-start.1 = ((bf16[128,8,128]{2,1,0:T(8,128)(2,1)}), bf16[128,8,128]{2,1,0:T(8,128)(2,1)S(1)}, u32[]{:S(2)}, u32[]{:S(2)}) async-start(bf16[128,8,128]{2,1,0:T(8,128)(2,1)} %get-tuple-element.43), calls=%async_computation.1 | async-start | bytes 524288 | tf_op jit(solution)/shard_map/all_to_all | solution.py:38
  69.0 0.3 collective-permute-start.6
  69.3 7.0 %collective-permute-start.7 = (bf16[80,512]{1,0:T(8,128)(2,1)}, bf16[80,512]{1,0:T(8,128)(2,1)S(1)}, u32[]{:S(2)}, u32[]{:S(2)}) collective-permute-start(bf16[80,512]{1,0:T(8,128)(2,1)} %get-tuple-element.38), channel_id=1, source_target_pairs={{0,126},{1,127},{2,0},{3,1},{4,2},{5,3},{6,4},{7,5},{8,6},{9,7},{1... | collective-permute-start | bytes 245768 | tf_op jit(solution)/shard_map/ppermute | solution.py:34
  76.3 0.9 collective-permute-start.8
  77.3 0.7 collective-permute-start.9
  78.0 1.3 %collective-permute-start.10 = (bf16[80,512]{1,0:T(8,128)(2,1)}, bf16[80,512]{1,0:T(8,128)(2,1)S(1)}, u32[]{:S(2)}, u32[]{:S(2)}) collective-permute-start(bf16[80,512]{1,0:T(8,128)(2,1)} %get-tuple-element.41), channel_id=1, source_target_pairs={{0,2},{1,3},{2,4},{3,5},{4,6},{5,7},{6,8},{7,9},{8,10},{9,11},{10,... | collective-permute-start | bytes 245768 | tf_op jit(solution)/shard_map/ppermute | solution.py:34
  79.3 0.0 collective-permute-done.6.n0
  79.3 0.0 copy-start.2
  79.3 1.0 %collective-permute-start.11 = (bf16[80,512]{1,0:T(8,128)(2,1)}, bf16[80,512]{1,0:T(8,128)(2,1)S(1)}, u32[]{:S(2)}, u32[]{:S(2)}) collective-permute-start(bf16[80,512]{1,0:T(8,128)(2,1)} %get-tuple-element.42), channel_id=1, source_target_pairs={{0,3},{1,4},{2,5},{3,6},{4,7},{5,8},{6,9},{7,10},{8,11},{9,12},{10... | collective-permute-start | bytes 245768 | tf_op jit(solution)/shard_map/ppermute | solution.py:34
  80.3 8.7 %shard_map.168 = (bf16[3072,512]{1,0:T(8,128)(2,1)}, f32[512,512]{1,0:T(8,128)}) custom-call(s32[24,128]{1,0:T(8,128)} %bitcast.6, s32[24,128]{1,0:T(8,128)} %bitcast.9, bf16[1536,512]{1,0:T(8,128)(2,1)} %w1_hbm.5, f32[512,512]{1,0:T(8,128)} %get-tuple-element.33.direct_hbm, bf16[3072,512]{1,0:T(8,128)(2,1)} %get-tuple-element.34.hgrad_hbm, ...), custom_call_target="tpu_custom_call" | custom-call | flops 268435456 | bytes 1048576 | tf_op jit(solution)/shard_map/pallas_call | solution.py:520
  88.9 0.0 copy-done.2
  88.9 0.0 collective-permute-done.7.n1
  89.0 0.0 copy-start.3
  89.0 0.0 collective-permute-done.8.n2
  89.0 0.0 copy-start.4
  89.0 0.0 collective-permute-done.9.n3
  89.0 0.0 copy-start.5
  89.0 0.0 collective-permute-done.10.n4
  89.0 0.0 copy-start.6
  89.0 0.6 collective-permute-done.11.n5
  89.6 0.0 copy-start.7
  89.6 0.0 all-to-all-done.1.far_hbm
  89.6 0.0 copy-start
  89.6 0.0 copy-done.3
  89.6 0.0 copy-done.4
  89.7 0.0 copy-done.5
  89.7 0.0 copy-done.6
  89.7 0.6 copy-done.7
  90.3 0.1 copy-done
  90.4 3.1 %shard_map.169 = bf16[512,512]{1,0:T(8,128)(2,1)} custom-call(s32[1,736]{1,0:T(1,128)} %list_hbm.3, f32[512,512]{1,0:T(8,128)} %get-tuple-element.36.owned_hbm, bf16[80,512]{1,0:T(8,128)(2,1)} %copy-done.2, bf16[80,512]{1,0:T(8,128)(2,1)} %copy-done.3, bf16[80,512]{1,0:T(8,128)(2,1)} %copy-done.4, bf16[80,512]{1,0:T(8,128)(2,1)} %copy-done.5, ...), custom_call_target="tpu_custom_call" | custom-call | flops 536870912 | bytes 3145728 | tf_op jit(solution)/shard_map/pallas_call | solution.py:526
Async XLA Ops:
  3.0 34.6 %all-to-all-start = ((bf16[128,8,128]{2,1,0:T(8,128)(2,1)}), bf16[128,8,128]{2,1,0:T(8,128)(2,1)S(1)}, u32[]{:S(2)}, u32[]{:S(2)}) async-start(bf16[128,8,128]{2,1,0:T(8,128)(2,1)} %get-tuple-element.30), calls=%async_computation | async-start | bytes 524288 | tf_op jit(solution)/shard_map/all_to_all | solution.py:38
  14.6 10.2 %collective-permute-start = (bf16[80,512]{1,0:T(8,128)(2,1)}, bf16[80,512]{1,0:T(8,128)(2,1)S(1)}, u32[]{:S(2)}, u32[]{:S(2)}) collective-permute-start(bf16[80,512]{1,0:T(8,128)(2,1)} %get-tuple-element.24), channel_id=1, source_target_pairs={{0,1},{1,2},{2,3},{3,4},{4,5},{5,6},{6,7},{7,8},{8,9},{9,10},{10,1... | collective-permute-start | bytes 245768 | tf_op jit(solution)/shard_map/ppermute | solution.py:34
  16.3 21.2 %collective-permute-start.1 = (bf16[80,512]{1,0:T(8,128)(2,1)}, bf16[80,512]{1,0:T(8,128)(2,1)S(1)}, u32[]{:S(2)}, u32[]{:S(2)}) collective-permute-start(bf16[80,512]{1,0:T(8,128)(2,1)} %get-tuple-element.25), channel_id=1, source_target_pairs={{0,2},{1,3},{2,4},{3,5},{4,6},{5,7},{6,8},{7,9},{8,10},{9,11},{10,... | collective-permute-start | bytes 245768 | tf_op jit(solution)/shard_map/ppermute | solution.py:34
  17.4 20.1 %collective-permute-start.2 = (bf16[80,512]{1,0:T(8,128)(2,1)}, bf16[80,512]{1,0:T(8,128)(2,1)S(1)}, u32[]{:S(2)}, u32[]{:S(2)}) collective-permute-start(bf16[80,512]{1,0:T(8,128)(2,1)} %get-tuple-element.26), channel_id=1, source_target_pairs={{0,3},{1,4},{2,5},{3,6},{4,7},{5,8},{6,9},{7,10},{8,11},{9,12},{10... | collective-permute-start | bytes 245768 | tf_op jit(solution)/shard_map/ppermute | solution.py:34
  19.1 18.4 %collective-permute-start.3 = (bf16[80,512]{1,0:T(8,128)(2,1)}, bf16[80,512]{1,0:T(8,128)(2,1)S(1)}, u32[]{:S(2)}, u32[]{:S(2)}) collective-permute-start(bf16[80,512]{1,0:T(8,128)(2,1)} %get-tuple-element.27), channel_id=1, source_target_pairs={{0,127},{1,0},{2,1},{3,2},{4,3},{5,4},{6,5},{7,6},{8,7},{9,8},{10,... | collective-permute-start | bytes 245768 | tf_op jit(solution)/shard_map/ppermute | solution.py:34
  19.1 18.4 %collective-permute-start.4 = (bf16[80,512]{1,0:T(8,128)(2,1)}, bf16[80,512]{1,0:T(8,128)(2,1)S(1)}, u32[]{:S(2)}, u32[]{:S(2)}) collective-permute-start(bf16[80,512]{1,0:T(8,128)(2,1)} %get-tuple-element.28), channel_id=1, source_target_pairs={{0,126},{1,127},{2,0},{3,1},{4,2},{5,3},{6,4},{7,5},{8,6},{9,7},{1... | collective-permute-start | bytes 245768 | tf_op jit(solution)/shard_map/ppermute | solution.py:34
  24.7 12.7 %copy-start.8 = (bf16[80,512]{1,0:T(8,128)(2,1)}, bf16[80,512]{1,0:T(8,128)(2,1)S(1)}, u32[]{:S(2)}) copy-start(bf16[80,512]{1,0:T(8,128)(2,1)S(1)} %collective-permute-done.n0) | copy-start | bytes 245764
  24.7 12.8 %collective-permute-start.5 = (bf16[80,512]{1,0:T(8,128)(2,1)}, bf16[80,512]{1,0:T(8,128)(2,1)S(1)}, u32[]{:S(2)}, u32[]{:S(2)}) collective-permute-start(bf16[80,512]{1,0:T(8,128)(2,1)} %get-tuple-element.29), channel_id=1, source_target_pairs={{0,125},{1,126},{2,127},{3,0},{4,1},{5,2},{6,3},{7,4},{8,5},{9,6},... | collective-permute-start | bytes 245768 | tf_op jit(solution)/shard_map/ppermute | solution.py:34
  37.5 0.6 copy-start.9
  37.5 0.6 copy-start.10
  37.5 0.7 copy-start.11
  37.6 0.7 copy-start.12
  37.6 0.7 copy-start.13
  37.6 0.7 copy-start.1
  65.3 24.4 %all-to-all-start.1 = ((bf16[128,8,128]{2,1,0:T(8,128)(2,1)}), bf16[128,8,128]{2,1,0:T(8,128)(2,1)S(1)}, u32[]{:S(2)}, u32[]{:S(2)}) async-start(bf16[128,8,128]{2,1,0:T(8,128)(2,1)} %get-tuple-element.43), calls=%async_computation.1 | async-start | bytes 524288 | tf_op jit(solution)/shard_map/all_to_all | solution.py:38
  69.0 10.2 %collective-permute-start.6 = (bf16[80,512]{1,0:T(8,128)(2,1)}, bf16[80,512]{1,0:T(8,128)(2,1)S(1)}, u32[]{:S(2)}, u32[]{:S(2)}) collective-permute-start(bf16[80,512]{1,0:T(8,128)(2,1)} %get-tuple-element.37), channel_id=1, source_target_pairs={{0,127},{1,0},{2,1},{3,2},{4,3},{5,4},{6,5},{7,6},{8,7},{9,8},{10,... | collective-permute-start | bytes 245768 | tf_op jit(solution)/shard_map/ppermute | solution.py:34
  69.3 19.6 %collective-permute-start.7 = (bf16[80,512]{1,0:T(8,128)(2,1)}, bf16[80,512]{1,0:T(8,128)(2,1)S(1)}, u32[]{:S(2)}, u32[]{:S(2)}) collective-permute-start(bf16[80,512]{1,0:T(8,128)(2,1)} %get-tuple-element.38), channel_id=1, source_target_pairs={{0,126},{1,127},{2,0},{3,1},{4,2},{5,3},{6,4},{7,5},{8,6},{9,7},{1... | collective-permute-start | bytes 245768 | tf_op jit(solution)/shard_map/ppermute | solution.py:34
  76.3 12.6 %collective-permute-start.8 = (bf16[80,512]{1,0:T(8,128)(2,1)}, bf16[80,512]{1,0:T(8,128)(2,1)S(1)}, u32[]{:S(2)}, u32[]{:S(2)}) collective-permute-start(bf16[80,512]{1,0:T(8,128)(2,1)} %get-tuple-element.39), channel_id=1, source_target_pairs={{0,125},{1,126},{2,127},{3,0},{4,1},{5,2},{6,3},{7,4},{8,5},{9,6},... | collective-permute-start | bytes 245768 | tf_op jit(solution)/shard_map/ppermute | solution.py:34
  77.3 11.7 %collective-permute-start.9 = (bf16[80,512]{1,0:T(8,128)(2,1)}, bf16[80,512]{1,0:T(8,128)(2,1)S(1)}, u32[]{:S(2)}, u32[]{:S(2)}) collective-permute-start(bf16[80,512]{1,0:T(8,128)(2,1)} %get-tuple-element.40), channel_id=1, source_target_pairs={{0,1},{1,2},{2,3},{3,4},{4,5},{5,6},{6,7},{7,8},{8,9},{9,10},{10,1... | collective-permute-start | bytes 245768 | tf_op jit(solution)/shard_map/ppermute | solution.py:34
  78.0 11.0 %collective-permute-start.10 = (bf16[80,512]{1,0:T(8,128)(2,1)}, bf16[80,512]{1,0:T(8,128)(2,1)S(1)}, u32[]{:S(2)}, u32[]{:S(2)}) collective-permute-start(bf16[80,512]{1,0:T(8,128)(2,1)} %get-tuple-element.41), channel_id=1, source_target_pairs={{0,2},{1,3},{2,4},{3,5},{4,6},{5,7},{6,8},{7,9},{8,10},{9,11},{10,... | collective-permute-start | bytes 245768 | tf_op jit(solution)/shard_map/ppermute | solution.py:34
  79.3 9.7 %copy-start.2 = (bf16[80,512]{1,0:T(8,128)(2,1)}, bf16[80,512]{1,0:T(8,128)(2,1)S(1)}, u32[]{:S(2)}) copy-start(bf16[80,512]{1,0:T(8,128)(2,1)S(1)} %collective-permute-done.6.n0) | copy-start | bytes 245764
  79.3 10.4 %collective-permute-start.11 = (bf16[80,512]{1,0:T(8,128)(2,1)}, bf16[80,512]{1,0:T(8,128)(2,1)S(1)}, u32[]{:S(2)}, u32[]{:S(2)}) collective-permute-start(bf16[80,512]{1,0:T(8,128)(2,1)} %get-tuple-element.42), channel_id=1, source_target_pairs={{0,3},{1,4},{2,5},{3,6},{4,7},{5,8},{6,9},{7,10},{8,11},{9,12},{10... | collective-permute-start | bytes 245768 | tf_op jit(solution)/shard_map/ppermute | solution.py:34
  89.0 0.7 copy-start.3
  89.0 0.7 copy-start.4
  89.0 0.7 copy-start.5
  89.0 0.7 copy-start.6
  89.6 0.6 copy-start.7
  89.6 0.7 copy-start
